TPU v7x, 128 devices: a whole 4x4x4 slice. The times are simulated.
128 devices in a mesh: pp: 8 (over z, x_hi), ep: 16 (over y, x_lo, core).
Axes of the slice: x: 4 (x_hi: 2, x_lo: 2; x = x_hi * 2 + x_lo), y: 4, z: 4, core: 2. Of those that a mesh axis runs over, the one named last changes fastest.
Arguments:
- fwd_in: bfloat16 [8, 1024, 3584], P('pp', 'ep'), may hold values from -100 to 100
- fwd_routes: int32 [8, 2, 1024, 2], P('pp', None, 'ep'), may hold values from 0 to 15, all different within a row; in each aligned block of 64 rows (0 to 63, 64 to 127, ..., all dimensions but the last counted through in order) at most 12 rows name the same one
- fwd_gates: float32 [8, 2, 1024, 2], P('pp', None, 'ep'), may hold values from 0.2 to 1.5
- bwd_grad: bfloat16 [8, 1024, 3584], P('pp', 'ep'), may hold values from -6 to 6
- bwd_saved: bfloat16 [8, 2, 1024, 3584], P('pp', None, 'ep'), may hold values from -100 to 100
- bwd_routes: int32 [8, 2, 1024, 2], P('pp', None, 'ep'), may hold values from 0 to 15, all different within a row; in each aligned block of 64 rows (0 to 63, 64 to 127, ..., all dimensions but the last counted through in order) at most 12 rows name the same one
- bwd_gates: float32 [8, 2, 1024, 2], P('pp', None, 'ep'), may hold values from 0.2 to 1.5
- norm_gain: float32 [8, 3584], P('pp'), may hold values from 0.1 to 1.9
- gate_w: bfloat16 [8, 16, 3584, 1024], P('pp', 'ep'), may hold values from -0.09375 to 0.09375
- up_w: bfloat16 [8, 16, 3584, 1024], P('pp', 'ep'), may hold values from -0.09375 to 0.09375
- down_w: bfloat16 [8, 16, 1024, 3584], P('pp', 'ep'), may hold values from -0.1875 to 0.1875
Outputs:
- fwd_out: bfloat16 [8, 2, 1024, 3584], P('pp', None, 'ep')
- bwd_out: bfloat16 [8, 2, 1024, 3584], P('pp', None, 'ep')
Inputs may be any that keep to these rules, and one draw needn't show every extreme that they name: `fwd_routes`: A row's 2 experts differ. In each aligned block of 64 rows (one device's rows for one section and tick) no expert is named by more than 12 rows, a bound that some block reaches. `bwd_routes`: A row's 2 experts differ. In each aligned block of 64 rows (one device's rows for one section and tick) no expert is named by more than 12 rows, a bound that some block reaches.
All inputs are finite; a program needn't handle non-finite values.
Results may differ from a plain program's by a relative error of at most 0.0079.
Values may be sent and summed in bfloat16 or wider, within the bound.
A program may use at most 128 MiB of HBM per device.

v0:
```python
import jax
import jax.numpy as jnp
from jax import lax
from jax.sharding import PartitionSpec as P

TICKS = 2


def from_behind(shard, axis, by):
    size = lax.axis_size(axis)
    pairs = [(i, i + by) for i in range(size) if 0 <= i + by < size]
    return lax.ppermute(shard, axis, pairs)


def normed(values, norm_gain):
    scale = lax.rsqrt(jnp.mean(values * values, -1, keepdims=True) + 1e-06)
    return values * scale * norm_gain


def expert_forward(inputs, gate_mat, up_mat, down_mat):
    gate_pre = jnp.dot(inputs, gate_mat, preferred_element_type=jnp.float32)
    up_pre = jnp.dot(inputs, up_mat, preferred_element_type=jnp.float32)
    gated = (gate_pre * jax.nn.sigmoid(gate_pre) * up_pre).astype(jnp.bfloat16)
    return jnp.dot(gated, down_mat, preferred_element_type=jnp.float32).astype(jnp.bfloat16)


def expert_backward(inputs, grads, gate_mat, up_mat, down_mat):
    gate_pre = jnp.dot(inputs, gate_mat, preferred_element_type=jnp.float32)
    up_pre = jnp.dot(inputs, up_mat, preferred_element_type=jnp.float32)
    sigmoid_gate = jax.nn.sigmoid(gate_pre)
    hidden_grad = lax.dot_general(
        grads, down_mat, (((1,), (1,)), ((), ())), preferred_element_type=jnp.float32
    )
    gate_grad = (
        hidden_grad * up_pre * sigmoid_gate * (1.0 + gate_pre * (1.0 - sigmoid_gate))
    ).astype(jnp.bfloat16)
    up_grad = (hidden_grad * gate_pre * sigmoid_gate).astype(jnp.bfloat16)
    result = lax.dot_general(
        gate_grad, gate_mat, (((1,), (1,)), ((), ())), preferred_element_type=jnp.float32
    )
    result = result + lax.dot_general(
        up_grad, up_mat, (((1,), (1,)), ((), ())), preferred_element_type=jnp.float32
    )
    return result.astype(jnp.bfloat16)


def slot_targets(routes, experts, capacity):
    flat_routes = routes.reshape(-1)
    expert_ids = jnp.arange(experts, dtype=jnp.int32)
    onehot = (flat_routes[:, None] == expert_ids[None, :]).astype(jnp.int32)
    before = jnp.cumsum(onehot, 0) - onehot
    slot_ids = jnp.sum(before * onehot, 1)
    return flat_routes * capacity + slot_ids


def fill_slots(targets, token_values, experts, capacity):
    width = token_values.shape[1]
    buffer = jnp.zeros((experts * capacity, width), jnp.bfloat16).at[targets].set(token_values)
    return buffer.reshape(experts, capacity, width)


def flat_rows(received):
    count_src, slots_src, width = received.shape
    return received.reshape(count_src * slots_src, width)


def on_device(
    fwd_in,
    fwd_routes,
    fwd_gates,
    bwd_grad,
    bwd_saved,
    bwd_routes,
    bwd_gates,
    norm_gain,
    gate_w,
    up_w,
    down_w,
):
    experts = lax.axis_size("ep")
    rows_here = fwd_in.shape[1]
    width = fwd_in.shape[2]
    topw = fwd_routes.shape[3]
    capacity = 3 * rows_here * topw // (2 * experts)
    gain_row = norm_gain[0]
    gate_mat = gate_w[0, 0]
    up_mat = up_w[0, 0]
    down_mat = down_w[0, 0]
    fwd_acts = fwd_in[0]
    cot = bwd_grad[0]
    fwd_ticks = []
    bwd_ticks = []
    for tick in range(TICKS):
        fwd_route = fwd_routes[0, tick]
        fwd_mix = fwd_gates[0, tick]
        fwd_normed = normed(fwd_acts.astype(jnp.float32), gain_row).astype(jnp.bfloat16)
        fwd_targets = slot_targets(fwd_route, experts, capacity)
        fwd_send = fill_slots(fwd_targets, jnp.repeat(fwd_normed, topw, axis=0), experts, capacity)
        saved = bwd_saved[0, tick]
        saved_float = saved.astype(jnp.float32)
        bwd_route = bwd_routes[0, tick]
        bwd_mix = bwd_gates[0, tick]
        saved_normed = normed(saved_float, gain_row).astype(jnp.bfloat16)
        scaled = (
            (bwd_mix[:, :, None] * cot.astype(jnp.float32)[:, None, :])
            .astype(jnp.bfloat16)
            .reshape(-1, width)
        )
        bwd_targets = slot_targets(bwd_route, experts, capacity)
        send_inputs = fill_slots(
            bwd_targets, jnp.repeat(saved_normed, topw, axis=0), experts, capacity
        )
        send_grads = fill_slots(bwd_targets, scaled, experts, capacity)
        run_received = lax.all_to_all(fwd_send, "ep", split_axis=0, concat_axis=0, tiled=True)
        run_outputs = expert_forward(flat_rows(run_received), gate_mat, up_mat, down_mat).reshape(
            run_received.shape
        )
        fwd_back = lax.all_to_all(run_outputs, "ep", split_axis=0, concat_axis=0, tiled=True)
        inputs = lax.all_to_all(send_inputs, "ep", split_axis=0, concat_axis=0, tiled=True)
        grads = lax.all_to_all(send_grads, "ep", split_axis=0, concat_axis=0, tiled=True)
        outputs = expert_backward(
            flat_rows(inputs), flat_rows(grads), gate_mat, up_mat, down_mat
        ).reshape(inputs.shape)
        bwd_back = lax.all_to_all(outputs, "ep", split_axis=0, concat_axis=0, tiled=True)
        fwd_assign = (
            fwd_back.reshape(-1, width)[fwd_targets]
            .reshape(rows_here, topw, width)
            .astype(jnp.float32)
        )
        mixed = (
            fwd_acts.astype(jnp.float32) + jnp.sum(fwd_mix[:, :, None] * fwd_assign, 1)
        ).astype(jnp.bfloat16)
        fwd_ticks.append(mixed)
        bwd_assign = (
            bwd_back.reshape(-1, width)[bwd_targets]
            .reshape(rows_here, topw, width)
            .astype(jnp.float32)
        )
        summed = jnp.sum(bwd_assign, 1)
        _, pullback = jax.vjp(lambda values: normed(values, gain_row), saved_float)
        input_cot = (cot.astype(jnp.float32) + pullback(summed)[0]).astype(jnp.bfloat16)
        bwd_ticks.append(input_cot)
        if tick + 1 < TICKS:
            fwd_acts = from_behind(mixed, "pp", 1)
            cot = from_behind(input_cot, "pp", -1)
    return (jnp.stack(fwd_ticks)[None], jnp.stack(bwd_ticks)[None])


def solution(mesh):
    in_specs = (
        P("pp", "ep", None),
        P("pp", None, "ep", None),
        P("pp", None, "ep", None),
        P("pp", "ep", None),
        P("pp", None, "ep", None),
        P("pp", None, "ep", None),
        P("pp", None, "ep", None),
        P("pp", None),
        P("pp", "ep", None, None),
        P("pp", "ep", None, None),
        P("pp", "ep", None, None),
    )
    out_specs = (P("pp", None, "ep", None), P("pp", None, "ep", None))
    return jax.shard_map(
        on_device, mesh=mesh, in_specs=in_specs, out_specs=out_specs, check_vma=False
    )
```

profile of v0, /device:TPU:1, one launch (start us, length us, event | category | flops | bytes accessed | tf_op | source)
XLA Modules:
  0.0 519.8 jit_solution(76425375932572344)
XLA Ops:
  6.3 2.3 scatter_custom_fusion.3
  10.0 7.0 %all-to-all-start.5 = ((bf16[16,12,3584]{2,1,0:T(8,128)(2,1)}), bf16[16,12,3584]{2,1,0:T(8,128)(2,1)S(1)}, u32[]{:S(2)}, u32[]{:S(2)}) async-start(bf16[16,12,3584]{2,1,0:T(8,128)(2,1)} %reshape.382), calls=%async_computation.5 | async-start | bytes 3670016 | tf_op jit(solution)/shard_map/all_to_all | solution.py:119
  19.3 3.4 mul.367
  22.7 3.3 scatter_custom_fusion.2
  27.4 14.0 %all-to-all-done.5 = bf16[16,12,3584]{2,1,0:T(8,128)(2,1)S(1)} async-done(((bf16[16,12,3584]{2,1,0:T(8,128)(2,1)}), bf16[16,12,3584]{2,1,0:T(8,128)(2,1)S(1)}, u32[]{:S(2)}, u32[]{:S(2)}) %all-to-all-start.5) | async-done | bytes 1376288 | tf_op jit(solution)/shard_map/all_to_all | solution.py:119
  41.4 5.7 %all-to-all-start.4 = ((bf16[16,12,3584]{2,1,0:T(8,128)(2,1)}), bf16[16,12,3584]{2,1,0:T(8,128)(2,1)}, u32[]{:S(2)}, u32[]{:S(2)}) async-start(bf16[16,12,3584]{2,1,0:T(8,128)(2,1)} %reshape.379), calls=%async_computation.4 | async-start | bytes 3670016 | tf_op jit(solution)/shard_map/all_to_all | solution.py:120
  47.4 5.6 %fusion.26 = f32[192,1024]{1,0:T(8,128)} fusion(bf16[192,3584]{1,0:T(8,128)(2,1)S(1)} %reshape.383, bf16[1,1,3584,1024]{3,2,1,0:T(8,128)(2,1)} %param.19), kind=kOutput, calls=%fused_computation.36 | convolution fusion | flops 1409286144 | bytes 9502720 | tf_op jit(solution)/shard_map/dot_general | solution.py:28
  53.0 18.4 %all-to-all-done.4 = bf16[16,12,3584]{2,1,0:T(8,128)(2,1)} async-done(((bf16[16,12,3584]{2,1,0:T(8,128)(2,1)}), bf16[16,12,3584]{2,1,0:T(8,128)(2,1)}, u32[]{:S(2)}, u32[]{:S(2)}) %all-to-all-start.4) | async-done | bytes 1376288 | tf_op jit(solution)/shard_map/all_to_all | solution.py:120
  71.4 2.4 reshape.380
  73.8 5.7 %fusion.2 = f32[192,1024]{1,0:T(8,128)S(1)} fusion(bf16[192,3584]{1,0:T(8,128)(2,1)S(1)} %reshape.380, bf16[1,1,1024,3584]{3,2,1,0:T(8,128)(2,1)} %param.21), kind=kOutput, calls=%fused_computation.12 | convolution fusion | flops 1409286144 | bytes 9502720 | tf_op jit(solution)/shard_map/dot_general | solution.py:31
  80.4 7.2 %fusion.12 = f32[192,3584]{1,0:T(8,128)} fusion(bf16[1,1,3584,1024]{3,2,1,0:T(8,128)(2,1)} %param.20, f32[192,1024]{1,0:T(8,128)S(1)} %fusion.2, f32[192,1024]{1,0:T(8,128)S(1)} %copy-done.18), kind=kOutput, calls=%fused_computation.22 | convolution fusion | flops 1410465792 | bytes 11665408 | tf_op jit(solution)/shard_map/dot_general | solution.py:41
  87.6 10.6 %fusion.41 = bf16[192,3584]{1,0:T(8,128)(2,1)S(1)} fusion(f32[192,3584]{1,0:T(8,128)} %fusion.12, bf16[1,1,3584,1024]{3,2,1,0:T(8,128)(2,1)} %param.19, f32[192,1024]{1,0:T(8,128)} %copy-done.20, bf16[192,3584]{1,0:T(8,128)(2,1)S(1)} %reshape.383, bf16[1,1,3584,1024]{3,2,1,0:T(8,128)(2,1)} %param.20, f32[192,1024]{1,0:T(8,128)} %fusion.26), kind=kOutput, calls=%fused_computation.45 | convolution fusion | flops 2821914624 | bytes 21757952 | tf_op jit(solution)/shard_map/dot_general | solution.py:38
  99.6 5.3 %all-to-all-start.6 = ((bf16[16,12,3584]{2,1,0:T(8,128)(2,1)}), bf16[16,12,3584]{2,1,0:T(8,128)(2,1)}, u32[]{:S(2)}, u32[]{:S(2)}) async-start(bf16[16,12,3584]{2,1,0:T(8,128)(2,1)} %reshape.384), calls=%async_computation.6 | async-start | bytes 3670016 | tf_op jit(solution)/shard_map/all_to_all | solution.py:124
  105.8 23.4 %all-to-all-done.6 = bf16[16,12,3584]{2,1,0:T(8,128)(2,1)} async-done(((bf16[16,12,3584]{2,1,0:T(8,128)(2,1)}), bf16[16,12,3584]{2,1,0:T(8,128)(2,1)}, u32[]{:S(2)}, u32[]{:S(2)}) %all-to-all-start.6) | async-done | bytes 1376288 | tf_op jit(solution)/shard_map/all_to_all | solution.py:124
  129.3 2.4 reshape.385
  132.7 2.4 reshape.398
  135.1 3.8 reduce_sum.166
  142.2 2.9 scatter_custom_fusion.5
  146.5 5.1 all-to-all-start.8
  153.4 32.7 %collective-permute-done.1 = bf16[64,3584]{1,0:T(8,128)(2,1)S(1)} collective-permute-done((bf16[64,3584]{1,0:T(8,128)(2,1)S(1)}, bf16[64,3584]{1,0:T(8,128)(2,1)S(1)}, u32[]{:S(2)}, u32[]{:S(2)}) %collective-permute-start.1) | collective-permute-done | bytes 458784 | tf_op jit(solution)/shard_map/ppermute | solution.py:12
  187.8 3.4 mul.396
  191.3 3.3 scatter_custom_fusion.4
  196.0 5.1 all-to-all-start.7
  201.1 2.4 reshape.390
  203.5 5.6 %fusion.22 = f32[192,1024]{1,0:T(8,128)} fusion(bf16[192,3584]{1,0:T(8,128)(2,1)S(1)} %reshape.390, bf16[1,1,3584,1024]{3,2,1,0:T(8,128)(2,1)} %param.19), kind=kOutput, calls=%fused_computation.32 | convolution fusion | flops 1409286144 | bytes 9502720 | tf_op jit(solution)/shard_map/dot_general | solution.py:28
  209.0 16.5 %all-to-all-done.7 = bf16[16,12,3584]{2,1,0:T(8,128)(2,1)} async-done(((bf16[16,12,3584]{2,1,0:T(8,128)(2,1)}), bf16[16,12,3584]{2,1,0:T(8,128)(2,1)}, u32[]{:S(2)}, u32[]{:S(2)}) %all-to-all-start.7) | async-done | bytes 1376288 | tf_op jit(solution)/shard_map/all_to_all | solution.py:120
  225.5 3.4 reshape.387
  228.9 6.1 %fusion = f32[192,1024]{1,0:T(8,128)S(1)} fusion(bf16[192,3584]{1,0:T(8,128)(2,1)} %reshape.387, bf16[1,1,1024,3584]{3,2,1,0:T(8,128)(2,1)} %param.21), kind=kOutput, calls=%fused_computation.10 | convolution fusion | flops 1409286144 | bytes 9502720 | tf_op jit(solution)/shard_map/dot_general | solution.py:31
  235.9 7.2 %fusion.8 = f32[192,3584]{1,0:T(8,128)} fusion(bf16[1,1,3584,1024]{3,2,1,0:T(8,128)(2,1)} %param.20, f32[192,1024]{1,0:T(8,128)S(1)} %fusion, f32[192,1024]{1,0:T(8,128)S(1)} %copy-done.19), kind=kOutput, calls=%fused_computation.18 | convolution fusion | flops 1410465792 | bytes 11665408 | tf_op jit(solution)/shard_map/dot_general | solution.py:41
  243.1 11.7 %fusion.38 = bf16[192,3584]{1,0:T(8,128)(2,1)} fusion(f32[192,3584]{1,0:T(8,128)} %fusion.8, bf16[1,1,3584,1024]{3,2,1,0:T(8,128)(2,1)} %param.19, f32[192,1024]{1,0:T(8,128)} %copy-done.21, bf16[192,3584]{1,0:T(8,128)(2,1)S(1)} %reshape.390, bf16[1,1,3584,1024]{3,2,1,0:T(8,128)(2,1)} %param.20, f32[192,1024]{1,0:T(8,128)} %fusion.22), kind=kOutput, calls=%fused_computation.44 | convolution fusion | flops 2821914624 | bytes 21757952 | tf_op jit(solution)/shard_map/dot_general | solution.py:38
  254.8 3.3 reshape.391
  258.1 5.7 %all-to-all-start.9 = ((bf16[16,12,3584]{2,1,0:T(8,128)(2,1)}), bf16[16,12,3584]{2,1,0:T(8,128)(2,1)}, u32[]{:S(2)}, u32[]{:S(2)}) async-start(bf16[16,12,3584]{2,1,0:T(8,128)(2,1)} %reshape.391), calls=%async_computation.9 | async-start | bytes 3670016 | tf_op jit(solution)/shard_map/all_to_all | solution.py:124
  265.0 23.2 %all-to-all-done.9 = bf16[16,12,3584]{2,1,0:T(8,128)(2,1)} async-done(((bf16[16,12,3584]{2,1,0:T(8,128)(2,1)}), bf16[16,12,3584]{2,1,0:T(8,128)(2,1)}, u32[]{:S(2)}, u32[]{:S(2)}) %all-to-all-start.9) | async-done | bytes 1376288 | tf_op jit(solution)/shard_map/all_to_all | solution.py:124
  288.1 2.4 reshape.392
  292.6 3.2 reshape.401
  295.8 3.7 reduce_sum.172
  301.2 3.2 reshape.438
  304.4 2.9 scatter_custom_fusion
  308.8 29.4 %all_to_all.50 = bf16[16,12,3584]{2,1,0:T(8,128)(2,1)} all-to-all(bf16[16,12,3584]{2,1,0:T(8,128)(2,1)} %reshape.370), channel_id=1, replica_groups=mesh['pp'=8,'ep'=16] {'ep'}, dimensions={0} | all-to-all | bytes 2752512 | tf_op jit(solution)/shard_map/all_to_all | solution.py:114
  338.1 2.4 reshape.371
  340.5 5.6 %fusion.30 = f32[192,1024]{1,0:T(8,128)} fusion(bf16[192,3584]{1,0:T(8,128)(2,1)S(1)} %reshape.371, bf16[1,1,3584,1024]{3,2,1,0:T(8,128)(2,1)} %param.19), kind=kOutput, calls=%fused_computation.40 | convolution fusion | flops 1409286144 | bytes 9502720 | tf_op jit(solution)/shard_map/dot_general | solution.py:21
  346.1 9.6 %fusion.44 = bf16[192,3584]{1,0:T(8,128)(2,1)} fusion(bf16[1,1,1024,3584]{3,2,1,0:T(8,128)(2,1)} %param.21, bf16[192,3584]{1,0:T(8,128)(2,1)S(1)} %reshape.371, bf16[1,1,3584,1024]{3,2,1,0:T(8,128)(2,1)} %param.20, f32[192,1024]{1,0:T(8,128)} %fusion.30), kind=kOutput, calls=%fused_computation.46 | convolution fusion | flops 2820440064 | bytes 18219008 | tf_op jit(solution)/shard_map/dot_general | solution.py:24
  355.6 3.3 reshape.372
  359.0 5.3 %all-to-all-start.1 = ((bf16[16,12,3584]{2,1,0:T(8,128)(2,1)}), bf16[16,12,3584]{2,1,0:T(8,128)(2,1)}, u32[]{:S(2)}, u32[]{:S(2)}) async-start(bf16[16,12,3584]{2,1,0:T(8,128)(2,1)} %reshape.372), calls=%async_computation.1 | async-start | bytes 3670016 | tf_op jit(solution)/shard_map/all_to_all | solution.py:118
  364.9 23.9 %all-to-all-done.1 = bf16[16,12,3584]{2,1,0:T(8,128)(2,1)} async-done(((bf16[16,12,3584]{2,1,0:T(8,128)(2,1)}), bf16[16,12,3584]{2,1,0:T(8,128)(2,1)}, u32[]{:S(2)}, u32[]{:S(2)}) %all-to-all-start.1) | async-done | bytes 1376288 | tf_op jit(solution)/shard_map/all_to_all | solution.py:118
  388.7 2.4 reshape.373
  391.1 2.0 gather_fusion
  393.2 3.2 reshape.394
  396.4 4.1 multiply_reduce_fusion.1
  402.3 5.9 %collective-permute-start = (bf16[64,3584]{1,0:T(8,128)(2,1)}, bf16[64,3584]{1,0:T(8,128)(2,1)}, u32[]{:S(2)}, u32[]{:S(2)}) collective-permute-start(bf16[64,3584]{1,0:T(8,128)(2,1)} %fusion.96), channel_id=1, source_target_pairs={{0,16},{16,32},{32,48},{48,64},{64,80},{80,96},{96,112},{1,17},{17... | collective-permute-start | bytes 1376264 | tf_op jit(solution)/shard_map/ppermute | solution.py:12
  408.7 7.8 %collective-permute-done = bf16[64,3584]{1,0:T(8,128)(2,1)} collective-permute-done((bf16[64,3584]{1,0:T(8,128)(2,1)}, bf16[64,3584]{1,0:T(8,128)(2,1)}, u32[]{:S(2)}, u32[]{:S(2)}) %collective-permute-start) | collective-permute-done | bytes 458784 | tf_op jit(solution)/shard_map/ppermute | solution.py:12
  417.8 2.3 fusion.139
  421.9 3.7 scatter_custom_fusion.1
  425.6 3.3 reshape.375
  428.9 6.0 %all-to-all-start.2 = ((bf16[16,12,3584]{2,1,0:T(8,128)(2,1)}), bf16[16,12,3584]{2,1,0:T(8,128)(2,1)}, u32[]{:S(2)}, u32[]{:S(2)}) async-start(bf16[16,12,3584]{2,1,0:T(8,128)(2,1)} %reshape.375), calls=%async_computation.2 | async-start | bytes 3670016 | tf_op jit(solution)/shard_map/all_to_all | solution.py:114
  435.4 24.1 %all-to-all-done.2 = bf16[16,12,3584]{2,1,0:T(8,128)(2,1)} async-done(((bf16[16,12,3584]{2,1,0:T(8,128)(2,1)}), bf16[16,12,3584]{2,1,0:T(8,128)(2,1)}, u32[]{:S(2)}, u32[]{:S(2)}) %all-to-all-start.2) | async-done | bytes 1376288 | tf_op jit(solution)/shard_map/all_to_all | solution.py:114
  459.5 2.4 reshape.376
  461.9 5.6 %fusion.28 = f32[192,1024]{1,0:T(8,128)} fusion(bf16[192,3584]{1,0:T(8,128)(2,1)S(1)} %reshape.376, bf16[1,1,3584,1024]{3,2,1,0:T(8,128)(2,1)} %param.19), kind=kOutput, calls=%fused_computation.38 | convolution fusion | flops 1409286144 | bytes 9502720 | tf_op jit(solution)/shard_map/dot_general | solution.py:21
  467.4 9.6 %fusion.47 = bf16[192,3584]{1,0:T(8,128)(2,1)} fusion(bf16[1,1,1024,3584]{3,2,1,0:T(8,128)(2,1)} %param.21, bf16[192,3584]{1,0:T(8,128)(2,1)S(1)} %reshape.376, bf16[1,1,3584,1024]{3,2,1,0:T(8,128)(2,1)} %param.20, f32[192,1024]{1,0:T(8,128)} %fusion.28), kind=kOutput, calls=%fused_computation.47 | convolution fusion | flops 2820440064 | bytes 18219008 | tf_op jit(solution)/shard_map/dot_general | solution.py:24
  477.0 3.3 reshape.377
  480.3 5.5 %all-to-all-start.3 = ((bf16[16,12,3584]{2,1,0:T(8,128)(2,1)}), bf16[16,12,3584]{2,1,0:T(8,128)(2,1)}, u32[]{:S(2)}, u32[]{:S(2)}) async-start(bf16[16,12,3584]{2,1,0:T(8,128)(2,1)} %reshape.377), calls=%async_computation.3 | async-start | bytes 3670016 | tf_op jit(solution)/shard_map/all_to_all | solution.py:118
  488.0 22.2 %all-to-all-done.3 = bf16[16,12,3584]{2,1,0:T(8,128)(2,1)} async-done(((bf16[16,12,3584]{2,1,0:T(8,128)(2,1)}), bf16[16,12,3584]{2,1,0:T(8,128)(2,1)}, u32[]{:S(2)}, u32[]{:S(2)}) %all-to-all-start.3) | async-done | bytes 1376288 | tf_op jit(solution)/shard_map/all_to_all | solution.py:118
  510.2 2.4 reshape.378
  514.9 2.5 multiply_reduce_fusion
  (132 shorter events, 44.7 us)
Async XLA Ops:
  10.0 7.1 %copy-start.16 = (f32[1,2,64,2]{2,3,1,0:T(2,128)S(1)}, f32[1,2,64,2]{2,3,1,0:T(2,128)}, u32[]{:S(2)}) copy-start(f32[1,2,64,2]{2,3,1,0:T(2,128)} %param.17) | copy-start | bytes 3076
  10.0 7.3 %copy-start.8 = (bf16[1,64,3584]{2,1,0:T(8,128)(2,1)S(1)}, bf16[1,64,3584]{2,1,0:T(8,128)(2,1)}, u32[]{:S(2)}) copy-start(bf16[1,64,3584]{2,1,0:T(8,128)(2,1)} %param.14) | copy-start | bytes 1376260
  10.0 31.4 %all-to-all-start.5 = ((bf16[16,12,3584]{2,1,0:T(8,128)(2,1)}), bf16[16,12,3584]{2,1,0:T(8,128)(2,1)S(1)}, u32[]{:S(2)}, u32[]{:S(2)}) async-start(bf16[16,12,3584]{2,1,0:T(8,128)(2,1)} %reshape.382), calls=%async_computation.5 | async-start | bytes 3670016 | tf_op jit(solution)/shard_map/all_to_all | solution.py:119
  41.4 30.0 %all-to-all-start.4 = ((bf16[16,12,3584]{2,1,0:T(8,128)(2,1)}), bf16[16,12,3584]{2,1,0:T(8,128)(2,1)}, u32[]{:S(2)}, u32[]{:S(2)}) async-start(bf16[16,12,3584]{2,1,0:T(8,128)(2,1)} %reshape.379), calls=%async_computation.4 | async-start | bytes 3670016 | tf_op jit(solution)/shard_map/all_to_all | solution.py:120
  73.8 6.6 %copy-start.18 = (f32[192,1024]{1,0:T(8,128)S(1)}, f32[192,1024]{1,0:T(8,128)}, u32[]{:S(2)}) copy-start(f32[192,1024]{1,0:T(8,128)} %fusion.26) | copy-start | bytes 2359300
  79.5 0.9 copy-start.20
  99.6 29.7 %all-to-all-start.6 = ((bf16[16,12,3584]{2,1,0:T(8,128)(2,1)}), bf16[16,12,3584]{2,1,0:T(8,128)(2,1)}, u32[]{:S(2)}, u32[]{:S(2)}) async-start(bf16[16,12,3584]{2,1,0:T(8,128)(2,1)} %reshape.384), calls=%async_computation.6 | async-start | bytes 3670016 | tf_op jit(solution)/shard_map/all_to_all | solution.py:124
  135.1 3.8 copy-start
  135.1 4.1 copy-start.9
  146.5 5.2 copy-start.14
  146.5 49.5 %all-to-all-start.8 = ((bf16[16,12,3584]{2,1,0:T(8,128)(2,1)}), bf16[16,12,3584]{2,1,0:T(8,128)(2,1)}, u32[]{:S(2)}, u32[]{:S(2)}) async-start(bf16[16,12,3584]{2,1,0:T(8,128)(2,1)} %reshape.389), calls=%async_computation.8 | async-start | bytes 3670016 | tf_op jit(solution)/shard_map/all_to_all | solution.py:119
  151.7 34.4 %collective-permute-start.1 = (bf16[64,3584]{1,0:T(8,128)(2,1)S(1)}, bf16[64,3584]{1,0:T(8,128)(2,1)S(1)}, u32[]{:S(2)}, u32[]{:S(2)}) collective-permute-start(bf16[64,3584]{1,0:T(8,128)(2,1)S(1)} %copy-done.14), channel_id=1, source_target_pairs={{16,0},{32,16},{48,32},{64,48},{80,64},{96,80},{112,96},{17,1},{33... | collective-permute-start | bytes 1376264 | tf_op jit(solution)/shard_map/ppermute | solution.py:12
  186.1 1.7 copy-start.13
  196.0 29.5 %all-to-all-start.7 = ((bf16[16,12,3584]{2,1,0:T(8,128)(2,1)}), bf16[16,12,3584]{2,1,0:T(8,128)(2,1)}, u32[]{:S(2)}, u32[]{:S(2)}) async-start(bf16[16,12,3584]{2,1,0:T(8,128)(2,1)} %reshape.386), calls=%async_computation.7 | async-start | bytes 3670016 | tf_op jit(solution)/shard_map/all_to_all | solution.py:120
  228.9 7.0 %copy-start.19 = (f32[192,1024]{1,0:T(8,128)S(1)}, f32[192,1024]{1,0:T(8,128)}, u32[]{:S(2)}) copy-start(f32[192,1024]{1,0:T(8,128)} %fusion.22) | copy-start | bytes 2359300
  235.0 0.9 copy-start.21
  258.1 5.7 %copy-start.15 = (s32[1,2,64,2]{2,3,1,0:T(2,128)S(1)}, s32[1,2,64,2]{2,3,1,0:T(2,128)}, u32[]{:S(2)}) copy-start(s32[1,2,64,2]{2,3,1,0:T(2,128)} %param.12) | copy-start | bytes 3076
  258.1 6.7 %copy-start.5 = (bf16[1,64,3584]{2,1,0:T(8,128)(2,1)S(1)}, bf16[1,64,3584]{2,1,0:T(8,128)(2,1)}, u32[]{:S(2)}) copy-start(bf16[1,64,3584]{2,1,0:T(8,128)(2,1)} %param.11) | copy-start | bytes 1376260
  258.1 30.1 %all-to-all-start.9 = ((bf16[16,12,3584]{2,1,0:T(8,128)(2,1)}), bf16[16,12,3584]{2,1,0:T(8,128)(2,1)}, u32[]{:S(2)}, u32[]{:S(2)}) async-start(bf16[16,12,3584]{2,1,0:T(8,128)(2,1)} %reshape.391), calls=%async_computation.9 | async-start | bytes 3670016 | tf_op jit(solution)/shard_map/all_to_all | solution.py:124
  295.8 3.7 copy-start.6
  299.5 1.7 copy-start.1
  359.0 5.5 %copy-start.17 = (f32[1,2,64,2]{2,3,1,0:T(2,128)S(1)}, f32[1,2,64,2]{2,3,1,0:T(2,128)}, u32[]{:S(2)}) copy-start(f32[1,2,64,2]{2,3,1,0:T(2,128)} %param.13) | copy-start | bytes 3076
  359.0 29.8 %all-to-all-start.1 = ((bf16[16,12,3584]{2,1,0:T(8,128)(2,1)}), bf16[16,12,3584]{2,1,0:T(8,128)(2,1)}, u32[]{:S(2)}, u32[]{:S(2)}) async-start(bf16[16,12,3584]{2,1,0:T(8,128)(2,1)} %reshape.372), calls=%async_computation.1 | async-start | bytes 3670016 | tf_op jit(solution)/shard_map/all_to_all | solution.py:118
  396.4 5.1 copy-start.7
  400.5 0.9 copy-start.3
  401.4 16.4 %copy-start.2 = (f32[64,3584]{1,0:T(8,128)S(1)}, f32[64,3584]{1,0:T(8,128)}, u32[]{:S(2)}) copy-start(f32[64,3584]{1,0:T(8,128)} %copy-done.1) | copy-start | bytes 2752516
  402.3 14.2 %collective-permute-start = (bf16[64,3584]{1,0:T(8,128)(2,1)}, bf16[64,3584]{1,0:T(8,128)(2,1)}, u32[]{:S(2)}, u32[]{:S(2)}) collective-permute-start(bf16[64,3584]{1,0:T(8,128)(2,1)} %fusion.96), channel_id=1, source_target_pairs={{0,16},{16,32},{32,48},{48,64},{64,80},{80,96},{96,112},{1,17},{17... | collective-permute-start | bytes 1376264 | tf_op jit(solution)/shard_map/ppermute | solution.py:12
  428.9 6.2 %copy-start.10 = (bf16[1,64,3584]{2,1,0:T(8,128)(2,1)S(1)}, bf16[1,64,3584]{2,1,0:T(8,128)(2,1)}, u32[]{:S(2)}) copy-start(bf16[1,64,3584]{2,1,0:T(8,128)(2,1)} %param.14) | copy-start | bytes 1376260
  428.9 30.5 %all-to-all-start.2 = ((bf16[16,12,3584]{2,1,0:T(8,128)(2,1)}), bf16[16,12,3584]{2,1,0:T(8,128)(2,1)}, u32[]{:S(2)}, u32[]{:S(2)}) async-start(bf16[16,12,3584]{2,1,0:T(8,128)(2,1)} %reshape.375), calls=%async_computation.2 | async-start | bytes 3670016 | tf_op jit(solution)/shard_map/all_to_all | solution.py:114
  480.3 5.5 %copy-start.4 = (f32[64,3584]{1,0:T(8,128)S(1)}, f32[64,3584]{1,0:T(8,128)}, u32[]{:S(2)}) copy-start(f32[64,3584]{1,0:T(8,128)} %copy-done.3) | copy-start | bytes 2752516
  480.3 29.9 %all-to-all-start.3 = ((bf16[16,12,3584]{2,1,0:T(8,128)(2,1)}), bf16[16,12,3584]{2,1,0:T(8,128)(2,1)}, u32[]{:S(2)}, u32[]{:S(2)}) async-start(bf16[16,12,3584]{2,1,0:T(8,128)(2,1)} %reshape.377), calls=%async_computation.3 | async-start | bytes 3670016 | tf_op jit(solution)/shard_map/all_to_all | solution.py:118
  485.9 1.1 copy-start.11
  514.8 3.7 copy-start.12
where the time goes:
time: 529 us; the launch traced here: 520 us
  waiting for transfers between devices  206 us (39%)
  local copies, waits for them, and re-layouts  97.5 us (18%)
  matrix products  89.8 us (17%)
  starting transfers between devices  58.3 us (11%)
  other arithmetic  37.2 us (7%)
  blocking collectives  29.4 us (6%)
    all_to_all x2, waiting for transfers between devices, on_device(): lax.all_to_all(outputs, 'ep', split_axis=0, concat_axis=0, tiled=True)  46.6 us
    all_to_all x2, waiting for transfers between devices, on_device(): lax.all_to_all(run_outputs, 'ep', split_axis=0, concat_axis=0, tiled=True)  46.1 us
    ppermute x2, waiting for transfers between devices, from_behind(): return lax.ppermute(shard, axis, pairs)  40.5 us
    all_to_all x2, waiting for transfers between devices, on_device(): lax.all_to_all(send_grads, 'ep', split_axis=0, concat_axis=0, tiled=True)  34.9 us
    all_to_all x1, blocking collectives, on_device(): lax.all_to_all(fwd_send, 'ep', split_axis=0, concat_axis=0, tiled=True)  29.4 us
    all_to_all x1, waiting for transfers between devices, on_device(): lax.all_to_all(fwd_send, 'ep', split_axis=0, concat_axis=0, tiled=True)  24.1 us
    dot_general x2, matrix products, expert_backward(): lax.dot_general(gate_grad, gate_mat, (((1,), (1,)), ((), ())), preferred_...  22.2 us
    dot_general x2, matrix products, expert_forward(): jnp.dot(gated, down_mat, preferred_element_type=jnp.float32)  19.2 us
  transfers between devices with their start and end apart: 11, of which 10 were waited for; matrix products, arithmetic and copies ran while one was open for 8% of the time, Pallas kernels for 0%

commit v1 on v0

v1 whole, which is shorter than its diff:
```python
import jax
import jax.numpy as jnp
from jax import lax
from jax.experimental import pallas as pl
from jax.experimental.pallas import tpu as pltpu
from jax.sharding import PartitionSpec as P

MESH = pl.DeviceIdType.MESH
BF = jnp.bfloat16
F32 = jnp.float32

EP = 16
PP = 8
TOK = 64
CAP = 12
D = 3584
FH = 1024
ROWS = EP * CAP
BLK = 16
GRP = D // 4
WIDE = 3 * GRP
PACK = EP * BLK

F0D, B0S, B0C, F0R, B1S, B0R, F1D, B1C, F1R, B1R = range(10)


def dot(a, b):
    return jnp.dot(a, b, preferred_element_type=F32)


def dot_nt(a, b):
    return lax.dot_general(a, b, (((1,), (1,)), ((), ())), preferred_element_type=F32)


def iota(shape, dim):
    return lax.broadcasted_iota(jnp.int32, shape, dim)


def one_hot(cond):
    return jnp.where(cond, 1.0, 0.0).astype(BF)


def group(q):
    return pl.ds(pl.multiple_of(q * GRP, 128), GRP)


TAIL = pl.ds(WIDE, GRP)


def kernel(
    fwd_in,
    fwd_routes,
    fwd_gates,
    bwd_grad,
    bwd_saved,
    bwd_routes,
    bwd_gates,
    gain,
    gate_hbm,
    up_hbm,
    down_hbm,
    fwd_out,
    bwd_out,
    gate_w,
    up_w,
    down_w,
    fd_s,
    fd_r,
    fr_s,
    fr_r,
    bs_s,
    bs_r,
    bc_s,
    bc_r,
    br_s,
    br_r,
    mats,
    mats_t,
    unpk,
    pck,
    tok2,
    xs,
    cs,
    h1,
    h2,
    acts1,
    cot1,
    w_sem,
    s_sem,
    r_sem,
    rel_s,
    rel_r,
):
    pp = lax.axis_index("pp")
    me = lax.axis_index("ep")
    ahead = lax.rem(pp + 1, PP)
    behind = lax.rem(pp + PP - 1, PP)

    loads = [
        pltpu.make_async_copy(src, dst, w_sem.at[i])
        for i, (src, dst) in enumerate(
            ((gate_hbm, gate_w), (up_hbm, up_w), (down_hbm, down_w))
        )
    ]
    for load in loads:
        load.start()

    barrier = pltpu.get_barrier_semaphore()

    def greet(d, carry):
        pl.semaphore_signal(
            barrier, inc=1, device_id=(pp, lax.rem(me + d, EP)), device_id_type=MESH
        )
        return carry

    lax.fori_loop(1, EP, greet, 0)
    pl.semaphore_signal(barrier, inc=1, device_id=(ahead, me), device_id_type=MESH)
    pl.semaphore_signal(barrier, inc=1, device_id=(behind, me), device_id_type=MESH)

    def block(e):
        return pl.ds(pl.multiple_of(e * BLK, BLK), BLK)

    def exchange(src, dst, phase):
        pltpu.make_async_copy(
            src.at[block(me)], dst.at[block(me)], r_sem.at[phase]
        ).start()

        def one(d, carry):
            e = lax.rem(me + d, EP)
            pltpu.make_async_remote_copy(
                src_ref=src.at[block(e)],
                dst_ref=dst.at[block(me)],
                send_sem=s_sem.at[phase],
                recv_sem=r_sem.at[phase],
                device_id=(pp, e),
                device_id_type=MESH,
            ).start()
            return carry

        lax.fori_loop(1, EP, one, 0)

    def arrived(dst, phase):
        pltpu.make_async_copy(dst, dst, r_sem.at[phase]).wait()

    def left(src, phase):
        part = src.at[pl.ds(0, PACK - BLK)]
        pltpu.make_async_copy(part, part, s_sem.at[phase]).wait()

    def relay(src, dst, which, to):
        return pltpu.make_async_remote_copy(
            src_ref=src,
            dst_ref=dst,
            send_sem=rel_s.at[which],
            recv_sem=rel_r.at[which],
            device_id=(to, me),
            device_id_type=MESH,
        )

    def slots(routes, tick, p):
        both = routes[tick]
        expert = jnp.concatenate([both[:, 0:1], both[:, 1:2]], axis=0)
        lanes = iota((2 * TOK, 128), 1)
        chosen = one_hot(expert == lanes)
        lower = one_hot(iota((2 * TOK, 2 * TOK), 1) < iota((2 * TOK, 2 * TOK), 0))
        before = dot(lower, chosen)
        slot = jnp.sum(before * chosen.astype(F32), axis=1, keepdims=True).astype(
            jnp.int32
        )
        third = (
            jnp.where(slot >= 3, 1, 0)
            + jnp.where(slot >= 6, 1, 0)
            + jnp.where(slot >= 9, 1, 0)
        )
        rest = slot - 3 * third
        cols = iota((2 * TOK, PACK), 1)
        main = jnp.where(cols == expert * BLK + slot, 1.0, 0.0)
        for q in range(3):
            tail = jnp.where(
                cols == jnp.where(rest == q, expert * BLK + CAP + third, -1), 1.0, 0.0
            )
            full = jnp.concatenate([main, tail], axis=0)
            mats[p, q] = full.astype(BF)
            mats_t[p, q] = full.T.astype(BF)

    rows = iota((ROWS, PACK), 0)
    cols = iota((ROWS, PACK), 1)
    source, slot = rows // CAP, rows % CAP
    for q in range(3):
        main = jnp.where(cols == source * BLK + slot, 1.0, 0.0)
        tail = jnp.where(
            (cols == source * BLK + CAP + slot // 3) & (slot % 3 == q), 1.0, 0.0
        )
        unpk[q, pl.ds(0, ROWS), :] = main.astype(BF)
        unpk[q, pl.ds(ROWS, ROWS), :] = tail.astype(BF)
    rows = iota((PACK, ROWS), 0)
    cols = iota((PACK, ROWS), 1)
    source, slot = cols // CAP, cols % CAP
    for q in range(3):
        main = jnp.where(rows == source * BLK + slot, 1.0, 0.0)
        tail = jnp.where(
            (rows == source * BLK + CAP + slot // 3) & (slot % 3 == q), 1.0, 0.0
        )
        pck[q] = jnp.concatenate([main, tail], axis=1).astype(BF)

    def norm(values):
        scale = lax.rsqrt(jnp.mean(values * values, -1, keepdims=True) + 1e-06)
        return (values * scale * gain[...]).astype(BF)

    def fill(dst, p):
        def one(q, carry):
            both = jnp.concatenate([tok2[:, group(q)], tok2[:, TAIL]], axis=0)
            dst[:, group(q)] = dot(mats_t[p, q], both).astype(BF)
            return carry

        lax.fori_loop(0, 3, one, 0)

    def send_normed(values, dst, p):
        rounded = norm(values)
        tok2[pl.ds(0, TOK), :] = rounded
        tok2[pl.ds(TOK, TOK), :] = rounded
        fill(dst, p)

    def send_scaled(cot, gates, tick, dst, p):
        both = gates[tick]
        tok2[pl.ds(0, TOK), :] = (both[:, 0:1] * cot).astype(BF)
        tok2[pl.ds(TOK, TOK), :] = (both[:, 1:2] * cot).astype(BF)
        fill(dst, p)

    def unpack(src, dst):
        def one(q, tail):
            both = dot(unpk[q], src[:, group(q)])
            dst[:, group(q)] = both[:ROWS].astype(BF)
            return tail + both[ROWS:]

        tail = lax.fori_loop(0, 3, one, jnp.zeros((ROWS, GRP), F32))
        dst[:, TAIL] = tail.astype(BF)

    def pack(src, dst):
        def one(q, carry):
            both = jnp.concatenate([src[:, group(q)], src[:, TAIL]], axis=0)
            dst[:, group(q)] = dot(pck[q], both).astype(BF)
            return carry

        lax.fori_loop(0, 3, one, 0)

    def gather(src, p, take):
        def one(q, tail):
            both = dot(mats[p, q], src[:, group(q)])
            take(group(q), both[: 2 * TOK])
            return tail + both[2 * TOK :]

        take(TAIL, lax.fori_loop(0, 3, one, jnp.zeros((2 * TOK, GRP), F32)))

    def expert_forward():
        def hidden(n, carry):
            cut = pl.ds(pl.multiple_of(n * 256, 256), 256)
            gate_pre = dot(xs[...], gate_w[:, cut])
            up_pre = dot(xs[...], up_w[:, cut])
            h1[:, cut] = (gate_pre * jax.nn.sigmoid(gate_pre) * up_pre).astype(BF)
            return carry

        lax.fori_loop(0, FH // 256, hidden, 0)

        def outer(n, carry):
            cut = pl.ds(pl.multiple_of(n * 512, 512), 512)
            xs[:, cut] = dot(h1[...], down_w[:, cut]).astype(BF)
            return carry

        lax.fori_loop(0, D // 512, outer, 0)

    def expert_backward():
        def hidden(n, carry):
            cut = pl.ds(pl.multiple_of(n * 256, 256), 256)
            gate_pre = dot(xs[...], gate_w[:, cut])
            up_pre = dot(xs[...], up_w[:, cut])
            hidden_grad = dot_nt(cs[...], down_w[cut, :])
            sig = jax.nn.sigmoid(gate_pre)
            h1[:, cut] = (
                hidden_grad * up_pre * sig * (1.0 + gate_pre * (1.0 - sig))
            ).astype(BF)
            h2[:, cut] = (hidden_grad * gate_pre * sig).astype(BF)
            return carry

        lax.fori_loop(0, FH // 256, hidden, 0)

        def outer(n, carry):
            cut = pl.ds(pl.multiple_of(n * 512, 512), 512)
            xs[:, cut] = (
                dot_nt(h1[...], gate_w[cut, :]) + dot_nt(h2[...], up_w[cut, :])
            ).astype(BF)
            return carry

        lax.fori_loop(0, D // 512, outer, 0)

    def finish_forward(acts, tick, p):
        both = fwd_gates[tick]
        one, two = both[:, 0:1], both[:, 1:2]

        def take(cut, parts):
            mixed = one * parts[:TOK] + two * parts[TOK:]
            fwd_out[tick, :, cut] = (acts[:, cut].astype(F32) + mixed).astype(BF)

        gather(fr_r, p, take)

    def finish_backward(cot, tick, p, total):
        def take(cut, parts):
            total[:, cut] = parts[:TOK] + parts[TOK:]

        gather(br_r, p, take)
        saved = bwd_saved[tick].astype(F32)
        scale = lax.rsqrt(jnp.mean(saved * saved, -1, keepdims=True) + 1e-06)
        weighted = total[...] * gain[...]
        inner = jnp.sum(weighted * saved, -1, keepdims=True) * (1.0 / D)
        grad = weighted * scale - saved * (scale * scale * scale * inner)
        bwd_out[tick] = (cot[...].astype(F32) + grad).astype(BF)

    slots(fwd_routes, 0, 0)
    send_normed(fwd_in[...].astype(F32), fd_s, 0)
    pl.semaphore_wait(barrier, EP + 1)
    exchange(fd_s, fd_r, F0D)
    slots(bwd_routes, 0, 1)
    send_normed(bwd_saved[0].astype(F32), bs_s.at[0], 1)
    exchange(bs_s.at[0], bs_r.at[0], B0S)
    send_scaled(bwd_grad[...].astype(F32), bwd_gates, 0, bc_s, 1)
    exchange(bc_s, bc_r, B0C)
    slots(fwd_routes, 1, 2)
    slots(bwd_routes, 1, 3)
    send_normed(bwd_saved[1].astype(F32), bs_s.at[1], 3)
    for load in loads:
        load.wait()

    arrived(fd_r, F0D)
    unpack(fd_r, xs)
    expert_forward()
    pack(xs, fr_s)
    exchange(fr_s, fr_r, F0R)
    exchange(bs_s.at[1], bs_r.at[1], B1S)

    arrived(bs_r.at[0], B0S)
    unpack(bs_r.at[0], xs)
    arrived(bc_r, B0C)
    unpack(bc_r, cs)
    expert_backward()
    pack(xs, br_s)
    exchange(br_s, br_r, B0R)

    arrived(fr_r, F0R)
    finish_forward(fwd_in, 0, 0)
    forth = relay(fwd_out.at[0], acts1, 0, ahead)
    forth.start()
    left(fd_s, F0D)
    forth.wait_recv()

    acts1[...] = jnp.where(pp == 0, jnp.zeros_like(acts1), acts1[...])
    send_normed(acts1[...].astype(F32), fd_s, 2)
    exchange(fd_s, fd_r, F1D)

    def backward_total(total):
        arrived(br_r, B0R)
        finish_backward(bwd_grad, 0, 1, total)

    pl.run_scoped(backward_total, pltpu.VMEM((TOK, D), F32))
    back = relay(bwd_out.at[0], cot1, 1, behind)
    back.start()
    left(bc_s, B0C)
    back.wait_recv()
    cot1[...] = jnp.where(pp == PP - 1, jnp.zeros_like(cot1), cot1[...])
    send_scaled(cot1[...].astype(F32), bwd_gates, 1, bc_s, 3)
    exchange(bc_s, bc_r, B1C)

    arrived(fd_r, F1D)
    unpack(fd_r, xs)
    expert_forward()
    left(fr_s, F0R)
    pack(xs, fr_s)
    exchange(fr_s, fr_r, F1R)

    arrived(bs_r.at[1], B1S)
    unpack(bs_r.at[1], xs)
    arrived(bc_r, B1C)
    unpack(bc_r, cs)
    expert_backward()
    left(br_s, B0R)
    pack(xs, br_s)
    exchange(br_s, br_r, B1R)

    arrived(fr_r, F1R)
    finish_forward(acts1, 1, 2)

    def backward_last(total):
        arrived(br_r, B1R)
        finish_backward(cot1, 1, 3, total)

    pl.run_scoped(backward_last, pltpu.VMEM((TOK, D), F32))

    forth.wait_send()
    back.wait_send()
    left(bs_s.at[0], B0S)
    left(bs_s.at[1], B1S)
    left(fd_s, F1D)
    left(bc_s, B1C)
    left(fr_s, F1R)
    left(br_s, B1R)


def on_device(
    fwd_in,
    fwd_routes,
    fwd_gates,
    bwd_grad,
    bwd_saved,
    bwd_routes,
    bwd_gates,
    norm_gain,
    gate_w,
    up_w,
    down_w,
):
    vmem = pl.BlockSpec(memory_space=pltpu.VMEM)
    hbm = pl.BlockSpec(memory_space=pl.ANY)
    packed = pltpu.VMEM((PACK, WIDE), BF)
    packed2 = pltpu.VMEM((2, PACK, WIDE), BF)
    out = jax.ShapeDtypeStruct((2, TOK, D), BF)
    fwd, bwd = pl.pallas_call(
        kernel,
        out_shape=(out, out),
        in_specs=[vmem] * 8 + [hbm] * 3,
        out_specs=(vmem, vmem),
        scratch_shapes=[
            pltpu.VMEM((D, FH), BF),
            pltpu.VMEM((D, FH), BF),
            pltpu.VMEM((FH, D), BF),
            packed,
            packed,
            packed,
            packed,
            packed2,
            packed2,
            packed,
            packed,
            packed,
            packed,
            pltpu.VMEM((4, 3, 4 * TOK, PACK), BF),
            pltpu.VMEM((4, 3, PACK, 4 * TOK), BF),
            pltpu.VMEM((3, 2 * ROWS, PACK), BF),
            pltpu.VMEM((3, PACK, 2 * ROWS), BF),
            pltpu.VMEM((2 * TOK, D), BF),
            pltpu.VMEM((ROWS, D), BF),
            pltpu.VMEM((ROWS, D), BF),
            pltpu.VMEM((ROWS, FH), BF),
            pltpu.VMEM((ROWS, FH), BF),
            pltpu.VMEM((TOK, D), BF),
            pltpu.VMEM((TOK, D), BF),
            pltpu.SemaphoreType.DMA((3,)),
            pltpu.SemaphoreType.DMA((10,)),
            pltpu.SemaphoreType.DMA((10,)),
            pltpu.SemaphoreType.DMA((2,)),
            pltpu.SemaphoreType.DMA((2,)),
        ],
        compiler_params=pltpu.CompilerParams(
            collective_id=0, has_side_effects=True, vmem_limit_bytes=60 << 20
        ),
        cost_estimate=pl.CostEstimate(
            flops=2 * 2 * 8 * ROWS * D * FH,
            bytes_accessed=6 * D * FH,
            transcendentals=4 * ROWS * FH,
        ),
    )(
        fwd_in[0],
        fwd_routes[0],
        fwd_gates[0],
        bwd_grad[0],
        bwd_saved[0],
        bwd_routes[0],
        bwd_gates[0],
        norm_gain,
        gate_w[0, 0],
        up_w[0, 0],
        down_w[0, 0],
    )
    return fwd[None], bwd[None]


def solution(mesh):
    in_specs = (
        P("pp", "ep", None),
        P("pp", None, "ep", None),
        P("pp", None, "ep", None),
        P("pp", "ep", None),
        P("pp", None, "ep", None),
        P("pp", None, "ep", None),
        P("pp", None, "ep", None),
        P("pp", None),
        P("pp", "ep", None, None),
        P("pp", "ep", None, None),
        P("pp", "ep", None, None),
    )
    out_specs = (P("pp", None, "ep", None), P("pp", None, "ep", None))
    return jax.shard_map(
        on_device, mesh=mesh, in_specs=in_specs, out_specs=out_specs, check_vma=False
    )
```

time: 529 us -> 207 us (0.39); the launches traced: 520 us -> 204 us
  waiting for transfers between devices: 206 us -> 0 us
  Pallas kernels: 0 us -> 194 us
  matrix products: 89.8 us -> 0 us
  local copies, waits for them, and re-layouts: 97.5 us -> 9.97 us
  starting transfers between devices: 58.3 us -> 0 us
  other arithmetic: 37.2 us -> 0 us
  blocking collectives: 29.4 us -> 0 us
    pallas_call x0 -> x1, Pallas kernels: none -> 194 us  [on_device(): pl.pallas_call(kernel, out_shape=(out, out), in_specs=[vmem] * 8 + [hbm]...]
    all_to_all x9 -> x0, waiting for transfers between devices: 166 us -> none  [the longest x2 46.6 us: on_device(): lax.all_to_all(outputs, 'ep', split_axis=0, concat_axis=0, tiled=True)]
    dot_general x12 -> x0, matrix products: 89.8 us -> none  [the longest x2 22.2 us: expert_backward(): lax.dot_general(gate_grad, gate_mat, (((1,), (1,)), ((), ())), preferred_...]
    all_to_all x9 -> x0, starting transfers between devices: 50.8 us -> none  [the longest x2 12.2 us: on_device(): lax.all_to_all(send_inputs, 'ep', split_axis=0, concat_axis=0, tiled=True)]
    reshape x24 -> x0, local copies, waits for them, and re-layouts: 50.5 us -> none  [the longest x6 13.2 us: flat_rows(): return received.reshape(count_src * slots_src, width)]
    ppermute x2 -> x0, waiting for transfers between devices: 40.5 us -> none  [from_behind(): return lax.ppermute(shard, axis, pairs)]
    all_to_all x1 -> x0, blocking collectives: 29.4 us -> none  [on_device(): lax.all_to_all(fwd_send, 'ep', split_axis=0, concat_axis=0, tiled=True)]
    reduce_sum x13 -> x0, other arithmetic: 18 us -> none  [the longest x2 7.5 us: on_device(): summed = jnp.sum(bwd_assign, 1)]
  transfers between devices with their start and end apart: 11 -> 0, of which waited for: 10 -> 0; matrix products, arithmetic and copies ran while one was open for 8% -> 0% of each run, Pallas kernels for 0% -> 0%
where the time goes in v1:
time: 207 us; the launch traced here: 204 us
  Pallas kernels  194 us (94%)
  local copies, waits for them, and re-layouts  9.97 us (5%)
    pallas_call x1, Pallas kernels, on_device(): pl.pallas_call(kernel, out_shape=(out, out), in_specs=[vmem] * 8 + [hbm]...  194 us
    unnamed x6, local copies, waits for them, and re-layouts  9.97 us

profile of v1, /device:TPU:1, one launch (start us, length us, event | category | flops | bytes accessed | tf_op | source)
XLA Modules:
  0.0 204.2 jit_solution(10666580176880976684)
XLA Ops:
  0.6 1.4 copy.13
  2.0 1.4 copy.14
  3.5 1.4 copy.15
  4.9 1.4 copy.16
  6.3 193.6 %shard_map.122 = (bf16[2,64,3584]{2,1,0:T(8,128)(2,1)}, bf16[2,64,3584]{2,1,0:T(8,128)(2,1)}) custom-call(bf16[64,3584]{1,0:T(8,128)(2,1)} %bitcast.22, s32[2,64,2]{2,1,0:T(8,128)} %bitcast.14, f32[2,64,2]{2,1,0:T(8,128)} %bitcast.15, bf16[64,3584]{1,0:T(8,128)(2,1)} %bitcast.23, bf16[2,64,3584]{2,1,0:T(8,128)(2,1)} %bitcast.21, s32[2,64,2]{2,1,0:T(8,128)} %bitcast.16, ...), custom_call_target="tpu_custom_call" | custom-call | flops 22548578304 | bytes 22020096 | tf_op jit(solution)/shard_map/pallas_call | solution.py:424
  199.9 2.2 %copy.19 = bf16[1,2,64,3584]{3,2,1,0:T(8,128)(2,1)} copy(bf16[1,2,64,3584]{3,2,1,0:T(8,128)(2,1)} %bitcast.13) | data formatting | bytes 1835008
  202.0 2.2 %copy.20 = bf16[1,2,64,3584]{3,2,1,0:T(8,128)(2,1)} copy(bf16[1,2,64,3584]{3,2,1,0:T(8,128)(2,1)} %bitcast.12) | data formatting | bytes 1835008

commit v2 on v1

--- a/solution.py
+++ b/solution.py
@@ -20,6 +20,9 @@
 GRP = D // 4
 WIDE = 3 * GRP
 PACK = EP * BLK
+COL = EP // 2
+CAP2 = 2 * CAP
+BLK2 = 2 * BLK
 
 F0D, B0S, B0C, F0R, B1S, B0R, F1D, B1C, F1R, B1R = range(10)
 
@@ -76,25 +79,34 @@
     br_r,
     mats,
     mats_t,
+    mats_x,
     unpk,
+    unpk_x,
     pck,
-    tok2,
+    tok,
     xs,
     cs,
     h1,
     h2,
     acts1,
     cot1,
+    info_s,
+    info_r,
     w_sem,
     s_sem,
     r_sem,
     rel_s,
     rel_r,
+    inf_s,
+    inf_r,
 ):
     pp = lax.axis_index("pp")
     me = lax.axis_index("ep")
     ahead = lax.rem(pp + 1, PP)
     behind = lax.rem(pp + PP - 1, PP)
+    my_x = lax.rem(me // 2, 2)
+    beside = me + 2 - 4 * my_x
+    my_col = me // 4 * 2 + lax.rem(me, 2)
 
     loads = [
         pltpu.make_async_copy(src, dst, w_sem.at[i])
@@ -114,8 +126,11 @@
         return carry
 
     lax.fori_loop(1, EP, greet, 0)
-    pl.semaphore_signal(barrier, inc=1, device_id=(ahead, me), device_id_type=MESH)
-    pl.semaphore_signal(barrier, inc=1, device_id=(behind, me), device_id_type=MESH)
+    for section in (ahead, behind):
+        for place in (me, beside):
+            pl.semaphore_signal(
+                barrier, inc=1, device_id=(section, place), device_id_type=MESH
+            )
 
     def block(e):
         return pl.ds(pl.multiple_of(e * BLK, BLK), BLK)
@@ -139,26 +154,59 @@
 
         lax.fori_loop(1, EP, one, 0)
 
+    def block2(e):
+        return pl.ds(pl.multiple_of(e * BLK2, BLK2), BLK2)
+
+    def exchange_column(src, dst, phase):
+        pltpu.make_async_copy(
+            src.at[block2(my_col)], dst.at[block2(my_col)], r_sem.at[phase]
+        ).start()
+
+        def one(d, carry):
+            col = lax.rem(my_col + d, COL)
+            e = (col // 2 * 2 + my_x) * 2 + lax.rem(col, 2)
+            pltpu.make_async_remote_copy(
+                src_ref=src.at[block2(col)],
+                dst_ref=dst.at[block2(my_col)],
+                send_sem=s_sem.at[phase],
+                recv_sem=r_sem.at[phase],
+                device_id=(pp, e),
+                device_id_type=MESH,
+            ).start()
+            return carry
+
+        lax.fori_loop(1, COL, one, 0)
+
     def arrived(dst, phase):
         pltpu.make_async_copy(dst, dst, r_sem.at[phase]).wait()
 
-    def left(src, phase):
-        part = src.at[pl.ds(0, PACK - BLK)]
+    def left(src, phase, own=BLK):
+        part = src.at[pl.ds(0, PACK - own)]
         pltpu.make_async_copy(part, part, s_sem.at[phase]).wait()
 
     def relay(src, dst, which, to):
-        return pltpu.make_async_remote_copy(
-            src_ref=src,
-            dst_ref=dst,
-            send_sem=rel_s.at[which],
-            recv_sem=rel_r.at[which],
-            device_id=(to, me),
-            device_id_type=MESH,
-        )
-
-    def slots(routes, tick, p):
-        both = routes[tick]
-        expert = jnp.concatenate([both[:, 0:1], both[:, 1:2]], axis=0)
+        return [
+            pltpu.make_async_remote_copy(
+                src_ref=src,
+                dst_ref=dst.at[i],
+                send_sem=rel_s.at[which, i],
+                recv_sem=rel_r.at[which, i],
+                device_id=(to, place),
+                device_id_type=MESH,
+            )
+            for i, place in enumerate((me, beside))
+        ]
+
+    eye = iota((TOK, TOK), 0) == iota((TOK, TOK), 1)
+
+    def column(row):
+        return jnp.sum(jnp.where(eye, row, 0.0), axis=1, keepdims=True)
+
+    def columns(rows):
+        return column(rows[0:1]), column(rows[1:2])
+
+    def places(routes):
+        expert = jnp.concatenate(columns(routes), axis=0).astype(jnp.int32)
         lanes = iota((2 * TOK, 128), 1)
         chosen = one_hot(expert == lanes)
         lower = one_hot(iota((2 * TOK, 2 * TOK), 1) < iota((2 * TOK, 2 * TOK), 0))
@@ -171,16 +219,38 @@
             + jnp.where(slot >= 6, 1, 0)
             + jnp.where(slot >= 9, 1, 0)
         )
-        rest = slot - 3 * third
-        cols = iota((2 * TOK, PACK), 1)
-        main = jnp.where(cols == expert * BLK + slot, 1.0, 0.0)
+        return expert, slot, third, slot - 3 * third
+
+    lanes2 = iota((2 * TOK, PACK), 1)
+
+    def slots(routes, p):
+        expert, slot, third, rest = places(routes)
+        main = jnp.where(lanes2 == expert * BLK + slot, 1.0, 0.0)
         for q in range(3):
-            tail = jnp.where(
-                cols == jnp.where(rest == q, expert * BLK + CAP + third, -1), 1.0, 0.0
-            )
-            full = jnp.concatenate([main, tail], axis=0)
+            at = jnp.where(rest == q, expert * BLK + CAP + third, -1)
+            full = jnp.concatenate([main, jnp.where(lanes2 == at, 1.0, 0.0)], axis=0)
             mats[p, q] = full.astype(BF)
             mats_t[p, q] = full.T.astype(BF)
+
+    def slots_column(own, other, which):
+        parts = []
+        for s, routes in enumerate((own, other)):
+            expert, slot, third, rest = places(routes)
+            half = expert // 2
+            base = jnp.where(
+                half % 2 == my_x, (half // 2 * 2 + expert % 2) * BLK2, -(PACK * 2)
+            )
+            parts.append((base + s * CAP + slot, base + CAP2 + 4 * s + third, rest))
+        for q in range(3):
+            full = jnp.concatenate(
+                [jnp.where(lanes2 == at, 1.0, 0.0) for at, _, _ in parts]
+                + [
+                    jnp.where(lanes2 == jnp.where(rest == q, at, -1), 1.0, 0.0)
+                    for _, at, rest in parts
+                ],
+                axis=0,
+            )
+            mats_x[which, q] = full.T.astype(BF)
 
     rows = iota((ROWS, PACK), 0)
     cols = iota((ROWS, PACK), 1)
@@ -192,6 +262,15 @@
         )
         unpk[q, pl.ds(0, ROWS), :] = main.astype(BF)
         unpk[q, pl.ds(ROWS, ROWS), :] = tail.astype(BF)
+    other = jnp.where(source // 2 % 2 == my_x, 0, 1)
+    base = (source // 4 * 2 + source % 2) * BLK2
+    for q in range(3):
+        main = jnp.where(cols == base + other * CAP + slot, 1.0, 0.0)
+        tail = jnp.where(
+            (cols == base + CAP2 + 4 * other + slot // 3) & (slot % 3 == q), 1.0, 0.0
+        )
+        unpk_x[q, pl.ds(0, ROWS), :] = main.astype(BF)
+        unpk_x[q, pl.ds(ROWS, ROWS), :] = tail.astype(BF)
     rows = iota((PACK, ROWS), 0)
     cols = iota((PACK, ROWS), 1)
     source, slot = cols // CAP, cols % CAP
@@ -206,29 +285,31 @@
         scale = lax.rsqrt(jnp.mean(values * values, -1, keepdims=True) + 1e-06)
         return (values * scale * gain[...]).astype(BF)
 
-    def fill(dst, p):
+    def put(at, rows):
+        tok[pl.ds(at * TOK, TOK), :] = rows
+
+    def fill(dst, count, mat):
         def one(q, carry):
-            both = jnp.concatenate([tok2[:, group(q)], tok2[:, TAIL]], axis=0)
-            dst[:, group(q)] = dot(mats_t[p, q], both).astype(BF)
+            cut = pl.ds(0, count * TOK)
+            both = jnp.concatenate([tok[cut, group(q)], tok[cut, TAIL]], axis=0)
+            dst[:, group(q)] = dot(mat[q], both).astype(BF)
             return carry
 
         lax.fori_loop(0, 3, one, 0)
 
-    def send_normed(values, dst, p):
+    def put_normed(values, at):
         rounded = norm(values)
-        tok2[pl.ds(0, TOK), :] = rounded
-        tok2[pl.ds(TOK, TOK), :] = rounded
-        fill(dst, p)
-
-    def send_scaled(cot, gates, tick, dst, p):
-        both = gates[tick]
-        tok2[pl.ds(0, TOK), :] = (both[:, 0:1] * cot).astype(BF)
-        tok2[pl.ds(TOK, TOK), :] = (both[:, 1:2] * cot).astype(BF)
-        fill(dst, p)
-
-    def unpack(src, dst):
+        put(at, rounded)
+        put(at + 1, rounded)
+
+    def put_scaled(cot, gates, at):
+        one, two = columns(gates)
+        put(at, (one * cot).astype(BF))
+        put(at + 1, (two * cot).astype(BF))
+
+    def unpack(src, dst, maps):
         def one(q, tail):
-            both = dot(unpk[q], src[:, group(q)])
+            both = dot(maps[q], src[:, group(q)])
             dst[:, group(q)] = both[:ROWS].astype(BF)
             return tail + both[ROWS:]
 
@@ -292,15 +373,14 @@
 
         lax.fori_loop(0, D // 512, outer, 0)
 
-    def finish_forward(acts, tick, p):
-        both = fwd_gates[tick]
-        one, two = both[:, 0:1], both[:, 1:2]
+    def finish_forward(src, acts, tick, p):
+        one, two = columns(fwd_gates[tick])
 
         def take(cut, parts):
             mixed = one * parts[:TOK] + two * parts[TOK:]
             fwd_out[tick, :, cut] = (acts[:, cut].astype(F32) + mixed).astype(BF)
 
-        gather(fr_r, p, take)
+        gather(src, p, take)
 
     def finish_backward(cot, tick, p, total):
         def take(cut, parts):
@@ -314,46 +394,56 @@
         grad = weighted * scale - saved * (scale * scale * scale * inner)
         bwd_out[tick] = (cot[...].astype(F32) + grad).astype(BF)
 
-    slots(fwd_routes, 0, 0)
-    send_normed(fwd_in[...].astype(F32), fd_s, 0)
-    pl.semaphore_wait(barrier, EP + 1)
+    info_s[...] = jnp.zeros_like(info_s)
+    info_s[pl.ds(0, 2), pl.ds(0, TOK)] = fwd_routes[1].astype(F32)
+    info_s[pl.ds(2, 2), pl.ds(0, TOK)] = bwd_routes[1].astype(F32)
+    info_s[pl.ds(4, 2), pl.ds(0, TOK)] = bwd_gates[1]
+    inform = pltpu.make_async_remote_copy(
+        src_ref=info_s,
+        dst_ref=info_r,
+        send_sem=inf_s,
+        recv_sem=inf_r,
+        device_id=(pp, beside),
+        device_id_type=MESH,
+    )
+
+    slots(bwd_routes[0].astype(F32), 1)
+    put_normed(bwd_saved[0].astype(F32), 0)
+    fill(bs_s.at[0], 2, mats_t.at[1])
+    pl.semaphore_wait(barrier, EP + 3)
+    exchange(bs_s.at[0], bs_r.at[0], B0S)
+    put_scaled(bwd_grad[...].astype(F32), bwd_gates[0], 0)
+    fill(bc_s, 2, mats_t.at[1])
+    exchange(bc_s, bc_r, B0C)
+    inform.start()
+    slots(fwd_routes[0].astype(F32), 0)
+    put_normed(fwd_in[...].astype(F32), 0)
+    fill(fd_s, 2, mats_t.at[0])
     exchange(fd_s, fd_r, F0D)
-    slots(bwd_routes, 0, 1)
-    send_normed(bwd_saved[0].astype(F32), bs_s.at[0], 1)
-    exchange(bs_s.at[0], bs_r.at[0], B0S)
-    send_scaled(bwd_grad[...].astype(F32), bwd_gates, 0, bc_s, 1)
-    exchange(bc_s, bc_r, B0C)
-    slots(fwd_routes, 1, 2)
-    slots(bwd_routes, 1, 3)
-    send_normed(bwd_saved[1].astype(F32), bs_s.at[1], 3)
+    slots(fwd_routes[1].astype(F32), 2)
+    slots(bwd_routes[1].astype(F32), 3)
+    put_normed(bwd_saved[1].astype(F32), 0)
+    fill(bs_s.at[1], 2, mats_t.at[3])
+    inform.wait()
+    slots_column(info_s[0:2, 0:TOK], info_r[0:2, 0:TOK], 0)
+    slots_column(info_s[2:4, 0:TOK], info_r[2:4, 0:TOK], 1)
     for load in loads:
         load.wait()
 
+    left(bs_s.at[0], B0S)
+    arrived(bs_r.at[0], B0S)
+    unpack(bs_r.at[0], xs, unpk)
+    arrived(bc_r, B0C)
+    unpack(bc_r, cs, unpk)
+    expert_backward()
+    pack(xs, br_s)
+    exchange(br_s, br_r, B0R)
+
     arrived(fd_r, F0D)
-    unpack(fd_r, xs)
+    unpack(fd_r, xs, unpk)
     expert_forward()
     pack(xs, fr_s)
     exchange(fr_s, fr_r, F0R)
-    exchange(bs_s.at[1], bs_r.at[1], B1S)
-
-    arrived(bs_r.at[0], B0S)
-    unpack(bs_r.at[0], xs)
-    arrived(bc_r, B0C)
-    unpack(bc_r, cs)
-    expert_backward()
-    pack(xs, br_s)
-    exchange(br_s, br_r, B0R)
-
-    arrived(fr_r, F0R)
-    finish_forward(fwd_in, 0, 0)
-    forth = relay(fwd_out.at[0], acts1, 0, ahead)
-    forth.start()
-    left(fd_s, F0D)
-    forth.wait_recv()
-
-    acts1[...] = jnp.where(pp == 0, jnp.zeros_like(acts1), acts1[...])
-    send_normed(acts1[...].astype(F32), fd_s, 2)
-    exchange(fd_s, fd_r, F1D)
 
     def backward_total(total):
         arrived(br_r, B0R)
@@ -361,46 +451,74 @@
 
     pl.run_scoped(backward_total, pltpu.VMEM((TOK, D), F32))
     back = relay(bwd_out.at[0], cot1, 1, behind)
-    back.start()
+    for copy in back:
+        copy.start()
+    arrived(fr_r, F0R)
+    exchange(bs_s.at[1], bs_r.at[1], B1S)
+    finish_forward(fr_r, fwd_in, 0, 0)
+    forth = relay(fwd_out.at[0], acts1, 0, ahead)
+    for copy in forth:
+        copy.start()
+
     left(bc_s, B0C)
-    back.wait_recv()
+    for copy in back:
+        copy.wait_recv()
     cot1[...] = jnp.where(pp == PP - 1, jnp.zeros_like(cot1), cot1[...])
-    send_scaled(cot1[...].astype(F32), bwd_gates, 1, bc_s, 3)
-    exchange(bc_s, bc_r, B1C)
-
-    arrived(fd_r, F1D)
-    unpack(fd_r, xs)
-    expert_forward()
-    left(fr_s, F0R)
-    pack(xs, fr_s)
-    exchange(fr_s, fr_r, F1R)
+    put_scaled(cot1[0].astype(F32), bwd_gates[1], 0)
+    put_scaled(cot1[1].astype(F32), info_r[4:6, 0:TOK], 2)
+    fill(bc_s, 4, mats_x.at[1])
+    exchange_column(bc_s, bc_r, B1C)
+    left(fd_s, F0D)
+    for copy in forth:
+        copy.wait_recv()
+    acts1[...] = jnp.where(pp == 0, jnp.zeros_like(acts1), acts1[...])
+    put_normed(acts1[0].astype(F32), 0)
+    put_normed(acts1[1].astype(F32), 2)
+    fill(fd_s, 4, mats_x.at[0])
+    exchange_column(fd_s, fd_r, F1D)
 
     arrived(bs_r.at[1], B1S)
-    unpack(bs_r.at[1], xs)
+    unpack(bs_r.at[1], xs, unpk)
     arrived(bc_r, B1C)
-    unpack(bc_r, cs)
+    unpack(bc_r, cs, unpk_x)
     expert_backward()
     left(br_s, B0R)
     pack(xs, br_s)
     exchange(br_s, br_r, B1R)
 
-    arrived(fr_r, F1R)
-    finish_forward(acts1, 1, 2)
+    arrived(fd_r, F1D)
+    unpack(fd_r, xs, unpk_x)
+    expert_forward()
+    left(fr_s, F0R)
+    pack(xs, fr_s)
+    exchange(fr_s, bs_r.at[0], F1R)
 
     def backward_last(total):
         arrived(br_r, B1R)
-        finish_backward(cot1, 1, 3, total)
+        finish_backward(cot1.at[0], 1, 3, total)
 
     pl.run_scoped(backward_last, pltpu.VMEM((TOK, D), F32))
-
-    forth.wait_send()
-    back.wait_send()
-    left(bs_s.at[0], B0S)
+    arrived(bs_r.at[0], F1R)
+    finish_forward(bs_r.at[0], acts1.at[0], 1, 2)
+
+    for copy in forth + back:
+        copy.wait_send()
     left(bs_s.at[1], B1S)
-    left(fd_s, F1D)
-    left(bc_s, B1C)
+    left(fd_s, F1D, BLK2)
+    left(bc_s, B1C, BLK2)
     left(fr_s, F1R)
     left(br_s, B1R)
+
+
+def pass_on(fwd, bwd, fwd_out, bwd_out, sems):
+    copies = [
+        pltpu.make_async_copy(src, dst, sems.at[i])
+        for i, (src, dst) in enumerate(((fwd, fwd_out), (bwd, bwd_out)))
+    ]
+    for copy in copies:
+        copy.start()
+    for copy in copies:
+        copy.wait()
 
 
 def on_device(
@@ -421,9 +539,10 @@
     packed = pltpu.VMEM((PACK, WIDE), BF)
     packed2 = pltpu.VMEM((2, PACK, WIDE), BF)
     out = jax.ShapeDtypeStruct((2, TOK, D), BF)
+    kept = pltpu.VMEM((2, TOK, D), BF)
     fwd, bwd = pl.pallas_call(
         kernel,
-        out_shape=(out, out),
+        out_shape=(kept, kept),
         in_specs=[vmem] * 8 + [hbm] * 3,
         out_specs=(vmem, vmem),
         scratch_shapes=[
@@ -442,20 +561,26 @@
             packed,
             pltpu.VMEM((4, 3, 4 * TOK, PACK), BF),
             pltpu.VMEM((4, 3, PACK, 4 * TOK), BF),
+            pltpu.VMEM((2, 3, PACK, 8 * TOK), BF),
+            pltpu.VMEM((3, 2 * ROWS, PACK), BF),
             pltpu.VMEM((3, 2 * ROWS, PACK), BF),
             pltpu.VMEM((3, PACK, 2 * ROWS), BF),
-            pltpu.VMEM((2 * TOK, D), BF),
+            pltpu.VMEM((4 * TOK, D), BF),
             pltpu.VMEM((ROWS, D), BF),
             pltpu.VMEM((ROWS, D), BF),
             pltpu.VMEM((ROWS, FH), BF),
             pltpu.VMEM((ROWS, FH), BF),
-            pltpu.VMEM((TOK, D), BF),
-            pltpu.VMEM((TOK, D), BF),
+            pltpu.VMEM((2, TOK, D), BF),
+            pltpu.VMEM((2, TOK, D), BF),
+            pltpu.VMEM((8, 128), F32),
+            pltpu.VMEM((8, 128), F32),
             pltpu.SemaphoreType.DMA((3,)),
             pltpu.SemaphoreType.DMA((10,)),
             pltpu.SemaphoreType.DMA((10,)),
-            pltpu.SemaphoreType.DMA((2,)),
-            pltpu.SemaphoreType.DMA((2,)),
+            pltpu.SemaphoreType.DMA((2, 2)),
+            pltpu.SemaphoreType.DMA((2, 2)),
+            pltpu.SemaphoreType.DMA,
+            pltpu.SemaphoreType.DMA,
         ],
         compiler_params=pltpu.CompilerParams(
             collective_id=0, has_side_effects=True, vmem_limit_bytes=60 << 20
@@ -467,17 +592,25 @@
         ),
     )(
         fwd_in[0],
-        fwd_routes[0],
-        fwd_gates[0],
+        jnp.swapaxes(fwd_routes[0], 1, 2),
+        jnp.swapaxes(fwd_gates[0], 1, 2),
         bwd_grad[0],
         bwd_saved[0],
-        bwd_routes[0],
-        bwd_gates[0],
+        jnp.swapaxes(bwd_routes[0], 1, 2),
+        jnp.swapaxes(bwd_gates[0], 1, 2),
         norm_gain,
         gate_w[0, 0],
         up_w[0, 0],
         down_w[0, 0],
     )
+    fwd, bwd = pl.pallas_call(
+        pass_on,
+        out_shape=(out, out),
+        in_specs=[vmem] * 2,
+        out_specs=(hbm, hbm),
+        scratch_shapes=[pltpu.SemaphoreType.DMA((2,))],
+        compiler_params=pltpu.CompilerParams(vmem_limit_bytes=60 << 20),
+    )(*(pltpu.with_memory_space_constraint(a, pltpu.VMEM) for a in (fwd, bwd)))
     return fwd[None], bwd[None]
 
 

time: 207 us -> 180 us (0.87); the launches traced: 204 us -> 179 us
  Pallas kernels: 194 us -> 179 us
  local copies, waits for them, and re-layouts: 9.97 us -> 0 us
    pallas_call x1 -> x2, Pallas kernels: 194 us -> 179 us  [the longest x1 177 us: on_device(): pl.pallas_call(kernel, out_shape=(kept, kept), in_specs=[vmem] * 8 + [hbm...]
    unnamed x6 -> x0, local copies, waits for them, and re-layouts: 9.97 us -> none
where the time goes in v2:
time: 180 us; the launch traced here: 179 us
  Pallas kernels  179 us (99%)
    pallas_call x1, Pallas kernels, on_device(): pl.pallas_call(kernel, out_shape=(kept, kept), in_specs=[vmem] * 8 + [hbm...  177 us

profile of v2, /device:TPU:1, one launch (start us, length us, event | category | flops | bytes accessed | tf_op | source)
XLA Modules:
  0.0 179.5 jit_solution(15505422610357350081)
XLA Ops:
  0.6 177.4 %shard_map.122 = (bf16[2,64,3584]{2,1,0:T(8,128)(2,1)S(1)}, bf16[2,64,3584]{2,1,0:T(8,128)(2,1)S(1)}) custom-call(bf16[64,3584]{1,0:T(8,128)(2,1)} %bitcast.26, s32[2,2,64]{2,1,0:T(2,128)} %bitcast.28, f32[2,2,64]{2,1,0:T(2,128)} %bitcast.29, bf16[64,3584]{1,0:T(8,128)(2,1)} %bitcast.27, bf16[2,64,3584]{2,1,0:T(8,128)(2,1)} %bitcast.23, ...), custom_call_target="tpu_custom_call" | custom-call | flops 22548578304 | bytes 22020096 | tf_op jit(solution)/shard_map/pallas_call | solution.py:543
  178.1 1.2 shard_map.123

commit v3 on v2

--- a/solution.py
+++ b/solution.py
@@ -78,7 +78,6 @@
     br_s,
     br_r,
     mats,
-    mats_t,
     mats_x,
     unpk,
     unpk_x,
@@ -90,6 +89,9 @@
     h2,
     acts1,
     cot1,
+    near_s,
+    near_r,
+    fr2_r,
     info_s,
     info_r,
     w_sem,
@@ -99,6 +101,8 @@
     rel_r,
     inf_s,
     inf_r,
+    near_ss,
+    near_rs,
 ):
     pp = lax.axis_index("pp")
     me = lax.axis_index("ep")
@@ -127,10 +131,9 @@
 
     lax.fori_loop(1, EP, greet, 0)
     for section in (ahead, behind):
-        for place in (me, beside):
-            pl.semaphore_signal(
-                barrier, inc=1, device_id=(section, place), device_id_type=MESH
-            )
+        pl.semaphore_signal(
+            barrier, inc=1, device_id=(section, beside), device_id_type=MESH
+        )
 
     def block(e):
         return pl.ds(pl.multiple_of(e * BLK, BLK), BLK)
@@ -184,17 +187,42 @@
         part = src.at[pl.ds(0, PACK - own)]
         pltpu.make_async_copy(part, part, s_sem.at[phase]).wait()
 
+    def to_beside(src, dst, i):
+        return pltpu.make_async_remote_copy(
+            src_ref=src,
+            dst_ref=dst,
+            send_sem=near_ss.at[i],
+            recv_sem=near_rs.at[i],
+            device_id=(pp, beside),
+            device_id_type=MESH,
+        )
+
+    parts2 = tuple(pl.ds(i * TOK // 2, TOK // 2) for i in range(2))
+
     def relay(src, dst, which, to):
         return [
             pltpu.make_async_remote_copy(
-                src_ref=src,
-                dst_ref=dst.at[i],
+                src_ref=src.at[part],
+                dst_ref=dst.at[1, part],
                 send_sem=rel_s.at[which, i],
                 recv_sem=rel_r.at[which, i],
-                device_id=(to, place),
+                device_id=(to, beside),
                 device_id_type=MESH,
             )
-            for i, place in enumerate((me, beside))
+            for i, part in enumerate(parts2)
+        ]
+
+    def hand_on(dst, which):
+        return [
+            pltpu.make_async_remote_copy(
+                src_ref=dst.at[1, part],
+                dst_ref=dst.at[0, part],
+                send_sem=rel_s.at[which, 2 + i],
+                recv_sem=rel_r.at[which, 2 + i],
+                device_id=(pp, beside),
+                device_id_type=MESH,
+            )
+            for i, part in enumerate(parts2)
         ]
 
     eye = iota((TOK, TOK), 0) == iota((TOK, TOK), 1)
@@ -223,14 +251,15 @@
 
     lanes2 = iota((2 * TOK, PACK), 1)
 
-    def slots(routes, p):
+    def slots(routes, p, transposed=False):
         expert, slot, third, rest = places(routes)
         main = jnp.where(lanes2 == expert * BLK + slot, 1.0, 0.0)
         for q in range(3):
             at = jnp.where(rest == q, expert * BLK + CAP + third, -1)
             full = jnp.concatenate([main, jnp.where(lanes2 == at, 1.0, 0.0)], axis=0)
             mats[p, q] = full.astype(BF)
-            mats_t[p, q] = full.T.astype(BF)
+            if transposed:
+                mats_x[2, q, :, pl.ds(0, PACK)] = full.T.astype(BF)
 
     def slots_column(own, other, which):
         parts = []
@@ -382,11 +411,11 @@
 
         gather(src, p, take)
 
-    def finish_backward(cot, tick, p, total):
+    def finish_backward(src, cot, tick, p, total):
         def take(cut, parts):
             total[:, cut] = parts[:TOK] + parts[TOK:]
 
-        gather(br_r, p, take)
+        gather(src, p, take)
         saved = bwd_saved[tick].astype(F32)
         scale = lax.rsqrt(jnp.mean(saved * saved, -1, keepdims=True) + 1e-06)
         weighted = total[...] * gain[...]
@@ -395,9 +424,21 @@
         bwd_out[tick] = (cot[...].astype(F32) + grad).astype(BF)
 
     info_s[...] = jnp.zeros_like(info_s)
-    info_s[pl.ds(0, 2), pl.ds(0, TOK)] = fwd_routes[1].astype(F32)
-    info_s[pl.ds(2, 2), pl.ds(0, TOK)] = bwd_routes[1].astype(F32)
-    info_s[pl.ds(4, 2), pl.ds(0, TOK)] = bwd_gates[1]
+    for i, what in enumerate(
+        (
+            bwd_routes[0],
+            fwd_routes[0],
+            fwd_routes[1],
+            bwd_routes[1],
+            bwd_gates[0],
+            bwd_gates[1],
+        )
+    ):
+        info_s[pl.ds(2 * i, 2), pl.ds(0, TOK)] = what.astype(F32)
+
+    def known(ref, i):
+        return ref[2 * i : 2 * i + 2, 0:TOK]
+
     inform = pltpu.make_async_remote_copy(
         src_ref=info_s,
         dst_ref=info_r,
@@ -406,104 +447,130 @@
         device_id=(pp, beside),
         device_id_type=MESH,
     )
-
-    slots(bwd_routes[0].astype(F32), 1)
+    cots = to_beside(bwd_grad, near_r.at[0], 0)
+    forths = to_beside(near_s.at[0], near_r.at[1], 1)
+    laters = to_beside(near_s.at[1], near_r.at[0], 2)
+
+    def put_pair(own, other):
+        for k in range(2):
+            put(k, own)
+            put(2 + k, other)
+
+    slots(bwd_routes[0].astype(F32), 0, True)
     put_normed(bwd_saved[0].astype(F32), 0)
-    fill(bs_s.at[0], 2, mats_t.at[1])
-    pl.semaphore_wait(barrier, EP + 3)
-    exchange(bs_s.at[0], bs_r.at[0], B0S)
+    fill(bs_s, 2, mats_x.at[2, :, :, pl.ds(0, PACK)])
+    pl.semaphore_wait(barrier, EP + 1)
+    inform.start()
+    cots.start()
+    exchange(bs_s, bs_r.at[0], B0S)
+    near_s[0] = norm(fwd_in[...].astype(F32))
+    near_s[1] = norm(bwd_saved[1].astype(F32))
+    inform.wait()
+    slots_column(known(info_s, 0), known(info_r, 0), 0)
     put_scaled(bwd_grad[...].astype(F32), bwd_gates[0], 0)
-    fill(bc_s, 2, mats_t.at[1])
-    exchange(bc_s, bc_r, B0C)
-    inform.start()
-    slots(fwd_routes[0].astype(F32), 0)
-    put_normed(fwd_in[...].astype(F32), 0)
-    fill(fd_s, 2, mats_t.at[0])
-    exchange(fd_s, fd_r, F0D)
-    slots(fwd_routes[1].astype(F32), 2)
-    slots(bwd_routes[1].astype(F32), 3)
-    put_normed(bwd_saved[1].astype(F32), 0)
-    fill(bs_s.at[1], 2, mats_t.at[3])
-    inform.wait()
-    slots_column(info_s[0:2, 0:TOK], info_r[0:2, 0:TOK], 0)
-    slots_column(info_s[2:4, 0:TOK], info_r[2:4, 0:TOK], 1)
+    cots.wait_recv()
+    put_scaled(near_r[0].astype(F32), known(info_r, 4), 2)
+    fill(bc_s, 4, mats_x.at[0])
+    exchange_column(bc_s, bc_r, B0C)
+    forths.start()
+    for p in range(1, 4):
+        slots_column(known(info_s, p), known(info_r, p), p)
+        slots(known(info_s, p), p)
     for load in loads:
         load.wait()
-
-    left(bs_s.at[0], B0S)
+    forths.wait_recv()
+    put_pair(near_s[0], near_r[1])
+    fill(fd_s, 4, mats_x.at[1])
+
     arrived(bs_r.at[0], B0S)
     unpack(bs_r.at[0], xs, unpk)
     arrived(bc_r, B0C)
-    unpack(bc_r, cs, unpk)
+    exchange_column(fd_s, fd_r, F0D)
+    laters.start()
+    unpack(bc_r, cs, unpk_x)
     expert_backward()
     pack(xs, br_s)
     exchange(br_s, br_r, B0R)
 
     arrived(fd_r, F0D)
-    unpack(fd_r, xs, unpk)
+    unpack(fd_r, xs, unpk_x)
     expert_forward()
     pack(xs, fr_s)
     exchange(fr_s, fr_r, F0R)
 
     def backward_total(total):
         arrived(br_r, B0R)
-        finish_backward(bwd_grad, 0, 1, total)
+        finish_backward(br_r, bwd_grad, 0, 0, total)
 
     pl.run_scoped(backward_total, pltpu.VMEM((TOK, D), F32))
     back = relay(bwd_out.at[0], cot1, 1, behind)
     for copy in back:
         copy.start()
+    left(bs_s, B0S)
+    laters.wait_recv()
+    put_pair(near_s[1], near_r[0])
+    fill(bs_s, 4, mats_x.at[3])
+    exchange_column(bs_s, bs_r.at[1], B1S)
+    back_on = hand_on(cot1, 1)
+    for copy, on in zip(back, back_on):
+        copy.wait_recv()
+        on.start()
     arrived(fr_r, F0R)
-    exchange(bs_s.at[1], bs_r.at[1], B1S)
-    finish_forward(fr_r, fwd_in, 0, 0)
+    finish_forward(fr_r, fwd_in, 0, 1)
     forth = relay(fwd_out.at[0], acts1, 0, ahead)
     for copy in forth:
         copy.start()
 
-    left(bc_s, B0C)
-    for copy in back:
+    left(bc_s, B0C, BLK2)
+    for on in back_on:
+        on.wait_recv()
+    last = pp == PP - 1
+    cot1[0] = jnp.where(last, jnp.zeros((TOK, D), BF), cot1[0])
+    put_scaled(cot1[0].astype(F32), bwd_gates[1], 0)
+    put_scaled(jnp.where(last, 0.0, cot1[1].astype(F32)), known(info_r, 5), 2)
+    fill(bc_s, 4, mats_x.at[3])
+    exchange_column(bc_s, bc_r, B1C)
+    forth_on = hand_on(acts1, 0)
+    for copy, on in zip(forth, forth_on):
         copy.wait_recv()
-    cot1[...] = jnp.where(pp == PP - 1, jnp.zeros_like(cot1), cot1[...])
-    put_scaled(cot1[0].astype(F32), bwd_gates[1], 0)
-    put_scaled(cot1[1].astype(F32), info_r[4:6, 0:TOK], 2)
-    fill(bc_s, 4, mats_x.at[1])
-    exchange_column(bc_s, bc_r, B1C)
-    left(fd_s, F0D)
-    for copy in forth:
-        copy.wait_recv()
-    acts1[...] = jnp.where(pp == 0, jnp.zeros_like(acts1), acts1[...])
+        on.start()
+    left(fd_s, F0D, BLK2)
+    first = pp == 0
+    put_normed(jnp.where(first, 0.0, acts1[1].astype(F32)), 2)
+    for on in forth_on:
+        on.wait_recv()
+    acts1[0] = jnp.where(first, jnp.zeros((TOK, D), BF), acts1[0])
     put_normed(acts1[0].astype(F32), 0)
-    put_normed(acts1[1].astype(F32), 2)
-    fill(fd_s, 4, mats_x.at[0])
+    fill(fd_s, 4, mats_x.at[2])
     exchange_column(fd_s, fd_r, F1D)
 
     arrived(bs_r.at[1], B1S)
-    unpack(bs_r.at[1], xs, unpk)
+    unpack(bs_r.at[1], xs, unpk_x)
     arrived(bc_r, B1C)
     unpack(bc_r, cs, unpk_x)
     expert_backward()
     left(br_s, B0R)
     pack(xs, br_s)
-    exchange(br_s, br_r, B1R)
+    exchange(br_s, bs_r.at[0], B1R)
 
     arrived(fd_r, F1D)
     unpack(fd_r, xs, unpk_x)
     expert_forward()
     left(fr_s, F0R)
     pack(xs, fr_s)
-    exchange(fr_s, bs_r.at[0], F1R)
+    exchange(fr_s, fr2_r, F1R)
 
     def backward_last(total):
-        arrived(br_r, B1R)
-        finish_backward(cot1.at[0], 1, 3, total)
+        arrived(bs_r.at[0], B1R)
+        finish_backward(bs_r.at[0], cot1.at[0], 1, 3, total)
 
     pl.run_scoped(backward_last, pltpu.VMEM((TOK, D), F32))
-    arrived(bs_r.at[0], F1R)
-    finish_forward(bs_r.at[0], acts1.at[0], 1, 2)
-
-    for copy in forth + back:
+    arrived(fr2_r, F1R)
+    finish_forward(fr2_r, acts1.at[0], 1, 2)
+
+    for copy in forth + forth_on + back + back_on + [cots, forths, laters]:
         copy.wait_send()
-    left(bs_s.at[1], B1S)
+    left(bs_s, B1S, BLK2)
     left(fd_s, F1D, BLK2)
     left(bc_s, B1C, BLK2)
     left(fr_s, F1R)
@@ -553,15 +620,14 @@
             packed,
             packed,
             packed,
+            packed,
             packed2,
-            packed2,
             packed,
             packed,
             packed,
             packed,
             pltpu.VMEM((4, 3, 4 * TOK, PACK), BF),
-            pltpu.VMEM((4, 3, PACK, 4 * TOK), BF),
-            pltpu.VMEM((2, 3, PACK, 8 * TOK), BF),
+            pltpu.VMEM((4, 3, PACK, 8 * TOK), BF),
             pltpu.VMEM((3, 2 * ROWS, PACK), BF),
             pltpu.VMEM((3, 2 * ROWS, PACK), BF),
             pltpu.VMEM((3, PACK, 2 * ROWS), BF),
@@ -572,15 +638,20 @@
             pltpu.VMEM((ROWS, FH), BF),
             pltpu.VMEM((2, TOK, D), BF),
             pltpu.VMEM((2, TOK, D), BF),
-            pltpu.VMEM((8, 128), F32),
-            pltpu.VMEM((8, 128), F32),
+            pltpu.VMEM((2, TOK, D), BF),
+            pltpu.VMEM((2, TOK, D), BF),
+            packed,
+            pltpu.VMEM((16, 128), F32),
+            pltpu.VMEM((16, 128), F32),
             pltpu.SemaphoreType.DMA((3,)),
             pltpu.SemaphoreType.DMA((10,)),
             pltpu.SemaphoreType.DMA((10,)),
-            pltpu.SemaphoreType.DMA((2, 2)),
-            pltpu.SemaphoreType.DMA((2, 2)),
+            pltpu.SemaphoreType.DMA((2, 4)),
+            pltpu.SemaphoreType.DMA((2, 4)),
             pltpu.SemaphoreType.DMA,
             pltpu.SemaphoreType.DMA,
+            pltpu.SemaphoreType.DMA((3,)),
+            pltpu.SemaphoreType.DMA((3,)),
         ],
         compiler_params=pltpu.CompilerParams(
             collective_id=0, has_side_effects=True, vmem_limit_bytes=60 << 20

time: 180 us -> 174 us (0.967)
  Pallas kernels: 179 us -> 173 us
    pallas_call x1, Pallas kernels: 177 us -> 172 us  [on_device(): pl.pallas_call(kernel, out_shape=(kept, kept), in_specs=[vmem] * 8 + [hbm...]
where the time goes in v3:
time: 174 us
  Pallas kernels  173 us (99%)
    pallas_call x1, Pallas kernels, on_device(): pl.pallas_call(kernel, out_shape=(kept, kept), in_specs=[vmem] * 8 + [hbm...  172 us

profile of v3, /device:TPU:1, one launch (start us, length us, event | category | flops | bytes accessed | tf_op | source)
XLA Modules:
  0.0 174.0 jit_solution(11668373073748751039)
XLA Ops:
  0.6 172.0 %shard_map.122 = (bf16[2,64,3584]{2,1,0:T(8,128)(2,1)S(1)}, bf16[2,64,3584]{2,1,0:T(8,128)(2,1)S(1)}) custom-call(bf16[64,3584]{1,0:T(8,128)(2,1)} %bitcast.26, s32[2,2,64]{2,1,0:T(2,128)} %bitcast.28, f32[2,2,64]{2,1,0:T(2,128)} %bitcast.29, bf16[64,3584]{1,0:T(8,128)(2,1)} %bitcast.27, bf16[2,64,3584]{2,1,0:T(8,128)(2,1)} %bitcast.23, ...), custom_call_target="tpu_custom_call" | custom-call | flops 22548578304 | bytes 22020096 | tf_op jit(solution)/shard_map/pallas_call | solution.py:610
  172.6 1.2 shard_map.123

commit v4 on v3

--- a/solution.py
+++ b/solution.py
@@ -87,6 +87,8 @@
     cs,
     h1,
     h2,
+    gates,
+    ups,
     acts1,
     cot1,
     near_s,
@@ -331,8 +333,8 @@
         put(at, rounded)
         put(at + 1, rounded)
 
-    def put_scaled(cot, gates, at):
-        one, two = columns(gates)
+    def put_scaled(cot, weights, at):
+        one, two = columns(weights)
         put(at, (one * cot).astype(BF))
         put(at + 1, (two * cot).astype(BF))
 
@@ -378,11 +380,19 @@
 
         lax.fori_loop(0, D // 512, outer, 0)
 
+    def expert_values():
+        def hidden(n, carry):
+            cut = pl.ds(pl.multiple_of(n * 256, 256), 256)
+            gates[:, cut] = dot(xs[...], gate_w[:, cut])
+            ups[:, cut] = dot(xs[...], up_w[:, cut])
+            return carry
+
+        lax.fori_loop(0, FH // 256, hidden, 0)
+
     def expert_backward():
         def hidden(n, carry):
             cut = pl.ds(pl.multiple_of(n * 256, 256), 256)
-            gate_pre = dot(xs[...], gate_w[:, cut])
-            up_pre = dot(xs[...], up_w[:, cut])
+            gate_pre, up_pre = gates[:, cut], ups[:, cut]
             hidden_grad = dot_nt(cs[...], down_w[cut, :])
             sig = jax.nn.sigmoid(gate_pre)
             h1[:, cut] = (
@@ -487,6 +497,7 @@
     arrived(bc_r, B0C)
     exchange_column(fd_s, fd_r, F0D)
     laters.start()
+    expert_values()
     unpack(bc_r, cs, unpk_x)
     expert_backward()
     pack(xs, br_s)
@@ -546,6 +557,7 @@
 
     arrived(bs_r.at[1], B1S)
     unpack(bs_r.at[1], xs, unpk_x)
+    expert_values()
     arrived(bc_r, B1C)
     unpack(bc_r, cs, unpk_x)
     expert_backward()
@@ -636,6 +648,8 @@
             pltpu.VMEM((ROWS, D), BF),
             pltpu.VMEM((ROWS, FH), BF),
             pltpu.VMEM((ROWS, FH), BF),
+            pltpu.VMEM((ROWS, FH), F32),
+            pltpu.VMEM((ROWS, FH), F32),
             pltpu.VMEM((2, TOK, D), BF),
             pltpu.VMEM((2, TOK, D), BF),
             pltpu.VMEM((2, TOK, D), BF),
@@ -654,7 +668,7 @@
             pltpu.SemaphoreType.DMA((3,)),
         ],
         compiler_params=pltpu.CompilerParams(
-            collective_id=0, has_side_effects=True, vmem_limit_bytes=60 << 20
+            collective_id=0, has_side_effects=True, vmem_limit_bytes=61 << 20
         ),
         cost_estimate=pl.CostEstimate(
             flops=2 * 2 * 8 * ROWS * D * FH,

time: 174 us -> 174 us (level)
  no operation moved by 1% of the time
where the time goes in v4:
time: 174 us
  Pallas kernels  173 us (99%)
    pallas_call x1, Pallas kernels, on_device(): pl.pallas_call(kernel, out_shape=(kept, kept), in_specs=[vmem] * 8 + [hbm...  172 us

profile of v4, /device:TPU:1, one launch (start us, length us, event | category | flops | bytes accessed | tf_op | source)
XLA Modules:
  0.0 173.8 jit_solution(15298629539863448637)
XLA Ops:
  0.6 171.7 %shard_map.122 = (bf16[2,64,3584]{2,1,0:T(8,128)(2,1)S(1)}, bf16[2,64,3584]{2,1,0:T(8,128)(2,1)S(1)}) custom-call(bf16[64,3584]{1,0:T(8,128)(2,1)} %bitcast.26, s32[2,2,64]{2,1,0:T(2,128)} %bitcast.28, f32[2,2,64]{2,1,0:T(2,128)} %bitcast.29, bf16[64,3584]{1,0:T(8,128)(2,1)} %bitcast.27, bf16[2,64,3584]{2,1,0:T(8,128)(2,1)} %bitcast.23, ...), custom_call_target="tpu_custom_call" | custom-call | flops 22548578304 | bytes 22020096 | tf_op jit(solution)/shard_map/pallas_call | solution.py:622
  172.4 1.2 shard_map.123
